TPU v7x, 256 devices: a whole 4x4x8 slice. The times are simulated.
256 devices in a mesh: seq: 16 (over z_hi, x), tp: 16 (over z_lo, y, core).
Axes of the slice: x: 4, y: 4, z: 8 (z_hi: 4, z_lo: 2; z = z_hi * 2 + z_lo), core: 2. Of those that a mesh axis runs over, the one named last changes fastest.
Arguments:
- tokens: bfloat16 [12288, 1152], P('seq', 'tp'), may hold values from -6 to 6
- modulation: float32 [9, 1152], replicated, may hold values from -3 to 3
- spatial_qkv: bfloat16 [3, 1152, 1152], P(None, None, 'tp'), may hold values from -1 to 1
- spatial_out: bfloat16 [1152, 1152], P('tp'), may hold values from -0.1875 to 0.1875
- temporal_qkv: bfloat16 [3, 1152, 1152], P(None, None, 'tp'), may hold values from -1 to 1
- temporal_out: bfloat16 [1152, 1152], P('tp'), may hold values from -0.1875 to 0.1875
- mlp_in: bfloat16 [1152, 4608], P(None, 'tp'), may hold values from -0.1875 to 0.1875
- mlp_out: bfloat16 [4608, 1152], P('tp'), may hold values from -0.09375 to 0.09375
Outputs:
- result: bfloat16 [12288, 1152], P('seq', 'tp')
All inputs are finite; a program needn't handle non-finite values.
Results may differ from a plain program's by a relative error of at most 0.035.
Values may be sent and summed in bfloat16 or wider, within the bound.
A program may use at most 64 MiB of HBM per device.

v0:
```python
import jax
import jax.numpy as jnp
from jax import lax
from jax.sharding import PartitionSpec as P

HD = 72


norm_eps = 1e-06


def modulated(inputs, shift_row, scale_row):
    as_float = inputs.astype(jnp.float32)
    average = jnp.mean(as_float, axis=-1, keepdims=True)
    centred = as_float - average
    variance = jnp.mean(centred * centred, axis=-1, keepdims=True)
    normed = centred * lax.rsqrt(variance + norm_eps)
    return (normed * (1.0 + scale_row) + shift_row).astype(jnp.bfloat16)


def project_three(normed, weights):
    return [
        jnp.dot(normed, weights[proj_index], preferred_element_type=jnp.float32).astype(
            jnp.bfloat16
        )
        for proj_index in range(3)
    ]


def spatial_mix(queries, keys_in, values_in):
    row_count = queries.shape[0]
    heads_here = queries.shape[1] // HD

    def split_heads(tensor):
        return tensor.reshape(row_count, heads_here, HD).transpose(1, 0, 2)

    def one_head(triple):
        query_h, key_h, value_h = triple
        scores = lax.dot_general(
            query_h, key_h, (((1,), (1,)), ((), ())), preferred_element_type=jnp.float32
        ) * HD ** (-0.5)
        row_top = jnp.max(scores, axis=1, keepdims=True)
        raised = jnp.exp(scores - row_top)
        weights = (raised / jnp.sum(raised, axis=1, keepdims=True)).astype(jnp.bfloat16)
        return jnp.dot(weights, value_h, preferred_element_type=jnp.float32).astype(jnp.bfloat16)

    mixture = lax.map(
        one_head, (split_heads(queries), split_heads(keys_in), split_heads(values_in))
    )
    return mixture.transpose(1, 0, 2).reshape(row_count, heads_here * HD)


def temporal_mix(queries, keys_in, values_in):
    frames_n, places, full_width = queries.shape
    head_shape = (frames_n, places, full_width // HD, HD)
    query_f = queries.reshape(head_shape).astype(jnp.float32)
    key_f = keys_in.reshape(head_shape).astype(jnp.float32)
    value_f = values_in.reshape(head_shape).astype(jnp.float32)
    scores = jnp.einsum("fphd,gphd->phfg", query_f, key_f) * HD ** (-0.5)
    row_top = jnp.max(scores, axis=-1, keepdims=True)
    raised = jnp.exp(scores - row_top)
    weights = (raised / jnp.sum(raised, axis=-1, keepdims=True)).astype(jnp.bfloat16)
    mixture = jnp.einsum("phfg,gphd->fphd", weights.astype(jnp.float32), value_f)
    return mixture.astype(jnp.bfloat16).reshape(frames_n, places, full_width)


def feed_forward(gathered, shift_row, scale_row, mlp_in, mlp_out):
    normed = modulated(gathered, shift_row, scale_row)
    hidden = jax.nn.gelu(
        jnp.dot(normed, mlp_in, preferred_element_type=jnp.float32), approximate=True
    ).astype(jnp.bfloat16)
    return jnp.dot(hidden, mlp_out, preferred_element_type=jnp.float32)


def residual_add(base, gate_row, update):
    return (base.astype(jnp.float32) + gate_row * update).astype(jnp.bfloat16)


def per_device(
    tokens, modulation, spatial_qkv, spatial_out, temporal_qkv, temporal_out, mlp_in, mlp_out
):
    row_count = tokens.shape[0]
    local_width = tokens.shape[1]
    offset = lax.axis_index("tp") * local_width
    own_mod = lax.dynamic_slice_in_dim(modulation, offset, local_width, 1)
    whole_rows = lax.all_gather(tokens, "tp", axis=1, tiled=True)
    normed = modulated(whole_rows, modulation[0], modulation[1])
    queries, keys_in, values_in = project_three(normed, spatial_qkv)
    partial_value = jnp.dot(
        spatial_mix(queries, keys_in, values_in), spatial_out, preferred_element_type=jnp.float32
    )
    attended = lax.psum_scatter(
        partial_value.astype(jnp.bfloat16), "tp", scatter_dimension=1, tiled=True
    ).astype(jnp.float32)
    after_spatial = residual_add(tokens, own_mod[2], attended)
    gathered = lax.all_gather(after_spatial, "tp", axis=1, tiled=True)
    normed = modulated(gathered, modulation[3], modulation[4])
    projected = jnp.stack(project_three(normed, temporal_qkv)).reshape(3, 1, row_count, local_width)
    exchanged = lax.all_to_all(projected, "seq", split_axis=2, concat_axis=1, tiled=True)
    mixture = temporal_mix(exchanged[0], exchanged[1], exchanged[2])
    returned = lax.all_to_all(mixture, "seq", split_axis=0, concat_axis=1, tiled=True).reshape(
        row_count, local_width
    )
    partial_value = jnp.dot(returned, temporal_out, preferred_element_type=jnp.float32)
    attended = lax.psum_scatter(
        partial_value.astype(jnp.bfloat16), "tp", scatter_dimension=1, tiled=True
    ).astype(jnp.float32)
    after_temporal = residual_add(after_spatial, own_mod[5], attended)
    gathered = lax.all_gather(after_temporal, "tp", axis=1, tiled=True)
    partial_value = feed_forward(gathered, modulation[6], modulation[7], mlp_in, mlp_out)
    result = residual_add(
        after_temporal,
        own_mod[8],
        lax.psum_scatter(
            partial_value.astype(jnp.bfloat16), "tp", scatter_dimension=1, tiled=True
        ).astype(jnp.float32),
    )
    return result


def solution(mesh):
    return jax.shard_map(
        per_device,
        mesh=mesh,
        in_specs=(
            P("seq", "tp"),
            P(),
            P(None, None, "tp"),
            P("tp", None),
            P(None, None, "tp"),
            P("tp", None),
            P(None, "tp"),
            P("tp", None),
        ),
        out_specs=P("seq", "tp"),
        check_vma=False,
    )
```

profile of v0, /device:TPU:1, one launch (start us, length us, event | category | flops | bytes accessed | tf_op | source)
XLA Modules:
  0.0 387.7 jit_solution(6077455851814893611)
XLA Ops:
  6.5 0.0 copy-start
  6.5 0.0 all-gather.4.cloned.1.call-start
  6.5 0.7 all-gather.4.cloned.1.call-update
  7.3 0.0 reduce-scatter.4.cloned.1.call-start
  7.3 1.1 add_reduce_fusion
  8.5 41.0 %all-gather.4.cloned.1.call-done = bf16[768,1152]{0,1:T(8,128)(2,1)} async-done(((bf16[768,72]{0,1:T(8,128)(2,1)}), bf16[768,1152]{0,1:T(8,128)(2,1)}) %all-gather.4.cloned.1.call-update) | async-done | bytes 1769488 | tf_op jit(solution)/shard_map/all_gather | solution.py:86
  49.5 1.9 convert_reduce_fusion.2
  51.4 0.1 copy-done.1
  51.5 0.5 fusion.15
  52.0 0.7 fusion.18
  52.7 0.0 copy-done.6
  52.7 0.4 convolution_convert_fusion.7
  53.1 1.4 fusion.57
  54.6 2.4 convolution_multiply_fusion
  57.0 3.5 online-softmax
  60.5 0.0 copy-done.10
  60.5 2.9 convolution_convert_fusion.2
  63.4 0.0 reduce-scatter.4.cloned.1.call-update
  63.4 0.0 all-gather.6.cloned.1.call-start
  63.5 0.9 dynamic-slice_bitcast_fusion
  64.3 61.0 %reduce-scatter.4.cloned.1.call-done = bf16[768,72]{0,1:T(8,128)(2,1)} async-done(((bf16[768,1152]{0,1:T(8,128)(2,1)}), bf16[768,72]{0,1:T(8,128)(2,1)}) %reduce-scatter.4.cloned.1.call-update) | async-done | bytes 110608 | tf_op jit(solution)/shard_map/reduce_scatter | solution.py:92
  125.3 0.0 copy-done.8
  125.3 1.6 add_convert_fusion.2
  127.0 0.0 all-gather.6.cloned.1.call-update
  127.0 0.0 reduce-scatter.6.cloned.1.call-start
  127.0 37.9 %all-gather.6.cloned.1.call-done = bf16[768,1152]{0,1:T(8,128)(2,1)} async-done(((bf16[768,72]{0,1:T(8,128)(2,1)}), bf16[768,1152]{0,1:T(8,128)(2,1)}) %all-gather.6.cloned.1.call-update) | async-done | bytes 1769488 | tf_op jit(solution)/shard_map/all_gather | solution.py:96
  165.0 1.9 convert_reduce_fusion.1
  166.9 0.1 copy-done.2
  167.0 0.5 fusion.11
  167.5 0.7 fusion.14
  168.2 0.0 copy-done.7
  168.2 0.4 fusion.28
  168.6 0.4 fusion.29
  169.1 0.4 fusion.30
  169.5 0.6 copy.22
  170.1 1.1 reshape.113
  171.2 20.0 %all_to_all.8 = bf16[16,2,5184]{2,1,0:T(2,128)(2,1)S(1)} all-to-all(bf16[16,2,5184]{2,1,0:T(2,128)(2,1)S(1)} %reshape.113), channel_id=1, replica_groups=mesh['seq'=16,'tp'=16] {'seq'}, dimensions={0} | all-to-all | bytes 663552 | tf_op jit(solution)/shard_map/all_to_all | solution.py:99
  191.3 1.3 reshape.114
  192.6 0.8 fusion.79
  193.5 0.2 convolution_multiply_fusion.1
  193.7 0.0 copy-start.9
  193.7 0.3 fusion.80
  194.1 0.3 fusion.27
  194.4 0.0 copy-start.4
  194.5 0.1 copy.30
  194.5 16.0 %all_to_all.9 = bf16[16,48,72]{2,1,0:T(8,128)(2,1)S(1)} all-to-all(bf16[16,48,72]{2,1,0:T(8,128)(2,1)S(1)} %copy.30), channel_id=1, replica_groups=mesh['seq'=16,'tp'=16] {'seq'}, dimensions={0} | all-to-all | bytes 221184 | tf_op jit(solution)/shard_map/all_to_all | solution.py:101
  210.6 1.9 convolution_convert_fusion.1
  212.5 0.0 reduce-scatter.6.cloned.1.call-update
  212.5 0.0 all-gather.8.cloned.1.call-start
  212.5 58.3 %reduce-scatter.6.cloned.1.call-done = bf16[768,72]{0,1:T(8,128)(2,1)} async-done(((bf16[768,1152]{0,1:T(8,128)(2,1)}), bf16[768,72]{0,1:T(8,128)(2,1)}) %reduce-scatter.6.cloned.1.call-update) | async-done | bytes 110608 | tf_op jit(solution)/shard_map/reduce_scatter | solution.py:105
  270.9 0.0 copy-done.4
  270.9 1.6 add_convert_fusion.1
  272.5 0.0 all-gather.8.cloned.1.call-update
  272.5 0.0 reduce-scatter.8.cloned.1.call-start
  272.6 37.9 %all-gather.8.cloned.1.call-done = bf16[768,1152]{0,1:T(8,128)(2,1)} async-done(((bf16[768,72]{0,1:T(8,128)(2,1)}), bf16[768,1152]{0,1:T(8,128)(2,1)}) %all-gather.8.cloned.1.call-update) | async-done | bytes 1769488 | tf_op jit(solution)/shard_map/all_gather | solution.py:109
  310.5 1.9 convert_reduce_fusion
  312.4 0.1 copy-done.3
  312.5 0.5 fusion.7
  313.1 0.0 copy-start.5
  313.1 4.5 %convolution_convert_fusion = bf16[768,1152]{0,1:T(8,128)(2,1)} fusion(bf16[288,1152]{1,0:T(8,128)(2,1)S(1)} %copy-done, bf16[1152,288]{0,1:T(8,128)(2,1)} %param.14, bf16[768,1152]{0,1:T(8,128)(2,1)S(1)} %copy-done.3, f32[1152]{0:T(1024)S(1)} %get-tuple-element.25, f32[1152]{0:T(1024)S(1)} %get-tuple-element.13, f32[768]{0:T(1024)S(1)} %add_rsqrt_fusion, ...), kind=kOutput, calls=%fused_computation.25 | convolution fusion | flops 1027399680 | bytes 4881408 | tf_op jit(solution)/shard_map/dot_general | solution.py:72
  317.6 0.0 reduce-scatter.8.cloned.1.call-update
  317.6 61.6 %reduce-scatter.8.cloned.1.call-done = bf16[768,72]{0,1:T(8,128)(2,1)} async-done(((bf16[768,1152]{0,1:T(8,128)(2,1)}), bf16[768,72]{0,1:T(8,128)(2,1)}) %reduce-scatter.8.cloned.1.call-update) | async-done | bytes 110608 | tf_op jit(solution)/shard_map/reduce_scatter | solution.py:114
  379.2 0.0 copy-done.5
  379.2 1.6 add_convert_fusion
  (19 shorter events, 0.2 us)
Async XLA Ops:
  6.5 306.5 %copy-start = (bf16[288,1152]{1,0:T(8,128)(2,1)S(1)}, bf16[288,1152]{1,0:T(8,128)(2,1)}, u32[]{:S(2)}) copy-start(bf16[288,1152]{1,0:T(8,128)(2,1)} %param.15) | copy-start | bytes 1990660
  6.5 43.0 %all-gather.4.cloned.1.call-start = ((), (), s32[]{:S(2)}) async-start(), calls=%async_computation.5 | async-start | bytes 1880064 | tf_op jit(solution)/shard_map/all_gather | solution.py:86
  7.3 118.0 %reduce-scatter.4.cloned.1.call-start = ((), (), s32[]{:S(2)}) async-start(), calls=%async_computation.6 | async-start | bytes 1880064 | tf_op jit(solution)/shard_map/reduce_scatter | solution.py:92
  49.5 2.0 copy-start.1
  51.5 1.2 copy-start.6
  57.0 3.5 copy-start.10
  60.5 64.8 %copy-start.8 = (bf16[768,72]{0,1:T(8,128)(2,1)S(1)}, bf16[768,72]{0,1:T(8,128)(2,1)}, u32[]{:S(2)}) copy-start(bf16[768,72]{0,1:T(8,128)(2,1)} %param.8) | copy-start | bytes 331780
  63.4 101.5 %all-gather.6.cloned.1.call-start = ((), (), s32[]{:S(2)}) async-start(), calls=%async_computation.7 | async-start | bytes 1880064 | tf_op jit(solution)/shard_map/all_gather | solution.py:96
  127.0 143.9 %reduce-scatter.6.cloned.1.call-start = ((), (), s32[]{:S(2)}) async-start(), calls=%async_computation.8 | async-start | bytes 1880064 | tf_op jit(solution)/shard_map/reduce_scatter | solution.py:105
  165.0 2.0 copy-start.2
  167.0 1.2 copy-start.7
  193.7 16.8 %copy-start.9 = (bf16[72,1152]{1,0:T(8,128)(2,1)S(1)}, bf16[72,1152]{1,0:T(8,128)(2,1)}, u32[]{:S(2)}) copy-start(bf16[72,1152]{1,0:T(8,128)(2,1)} %param.13) | copy-start | bytes 497668
  194.4 76.4 %copy-start.4 = (bf16[768,72]{0,1:T(8,128)(2,1)S(1)}, bf16[768,72]{0,1:T(8,128)(2,1)}, u32[]{:S(2)}) copy-start(bf16[768,72]{0,1:T(8,128)(2,1)} %add_convert_fusion.2) | copy-start | bytes 331780
  212.5 98.0 %all-gather.8.cloned.1.call-start = ((), (), s32[]{:S(2)}) async-start(), calls=%async_computation.9 | async-start | bytes 1880064 | tf_op jit(solution)/shard_map/all_gather | solution.py:109
  272.5 106.7 %reduce-scatter.8.cloned.1.call-start = ((), (), s32[]{:S(2)}) async-start(), calls=%async_computation.10 | async-start | bytes 1880064 | tf_op jit(solution)/shard_map/reduce_scatter | solution.py:114
  310.5 2.0 copy-start.3
  313.1 66.2 %copy-start.5 = (bf16[768,72]{0,1:T(8,128)(2,1)S(1)}, bf16[768,72]{0,1:T(8,128)(2,1)}, u32[]{:S(2)}) copy-start(bf16[768,72]{0,1:T(8,128)(2,1)} %add_convert_fusion.1) | copy-start | bytes 331780
Sparse Core Ops, SparseCore 0:
  9.2 40.2 all-gather.3
  63.6 61.7 reduce-scatter.3
  127.3 37.6 all-gather.5
  212.6 58.2 reduce-scatter.5
  272.7 37.7 all-gather.7
  317.7 61.4 reduce-scatter.7
where the time goes:
time: 391 us; the launch traced here: 388 us
  waiting for transfers between devices  299 us (76%)
  blocking collectives  36.1 us (9%)
  matrix products  15.8 us (4%)
  other arithmetic  14.8 us (4%)
  between operations  13.7 us (4%)
  local copies, waits for them, and re-layouts  5.08 us (1%)
    reduce_scatter x3, waiting for transfers between devices, per_device(): lax.psum_scatter(partial_value.astype(jnp.bfloat16), 'tp', scatter_dimens...  181 us
    all_gather x1, waiting for transfers between devices, per_device(): whole_rows = lax.all_gather(tokens, 'tp', axis=1, tiled=True)  41 us
    all_gather x1, waiting for transfers between devices, per_device(): gathered = lax.all_gather(after_spatial, 'tp', axis=1, tiled=True)  37.9 us
    all_gather x1, waiting for transfers between devices, per_device(): gathered = lax.all_gather(after_temporal, 'tp', axis=1, tiled=True)  37.9 us
    all_to_all x1, blocking collectives, per_device(): lax.all_to_all(projected, 'seq', split_axis=2, concat_axis=1, tiled=True)  20 us
    all_to_all x1, blocking collectives, per_device(): lax.all_to_all(mixture, 'seq', split_axis=0, concat_axis=1, tiled=True)  16 us
  transfers between devices with their start and end apart: 6, of which 6 were waited for; matrix products, arithmetic and copies ran while one was open for 1% of the time, Pallas kernels for 0%

commit v1 on v0

v1 whole, which is shorter than its diff:
```python
import jax
import jax.numpy as jnp
from jax import lax
from jax.experimental import pallas as pl
from jax.experimental.pallas import tpu as pltpu
from jax.sharding import PartitionSpec as P

HD = 72
D = 1152
N = 16
ROWS = 768
BLK = 48
FFL = 288
PADW = 80
EPS = 1e-06
SCALE = HD ** (-0.5)
BF = jnp.bfloat16
F32 = jnp.float32


def remote(src, dst, send_sem, recv_sem, device):
    return pltpu.make_async_remote_copy(
        src_ref=src,
        dst_ref=dst,
        send_sem=send_sem,
        recv_sem=recv_sem,
        device_id=device,
        device_id_type=pl.DeviceIdType.MESH,
    )


def modulated(rows, shift, scale):
    average = jnp.mean(rows, axis=-1, keepdims=True)
    centred = rows - average
    variance = jnp.mean(centred * centred, axis=-1, keepdims=True)
    return (centred * lax.rsqrt(variance + EPS) * (1.0 + scale) + shift).astype(BF)


class Gather:
    def __init__(self, slot, send, recv, pos):
        self.slot, self.send, self.recv, self.pos = slot, send, recv, pos
        self.sent = 0
        self.pending = []
        s, z, y, c = pos
        self.up = lax.rem(y + 1 + 2 * c, 4)
        self.down = lax.rem(y + 3 - 2 * c, 4)
        self.far = lax.rem(y + 2, 4)

    def index(self, z, y, c):
        return z * 8 + y * 2 + c

    def push(self, origin, target):
        ref = self.slot(origin)
        s = self.pos[0]
        copy = remote(ref, ref, self.send.at[self.sent], self.recv.at[origin], (s, target))
        copy.start()
        self.sent += 1
        self.pending.append(copy)

    def await_block(self, origin):
        ref = self.slot(origin)
        s, z, y, c = self.pos
        remote(
            ref, ref, self.send.at[0], self.recv.at[origin], (s, self.index(z, y, 1 - c))
        ).wait_recv()

    def p0(self):
        s, z, y, c = self.pos
        own = self.index(z, y, c)
        self.push(own, self.index(1 - z, y, c))
        self.push(own, self.index(z, self.up, c))
        self.push(own, self.index(z, self.down, c))
        self.push(own, self.index(z, y, 1 - c))

    def p1(self):
        s, z, y, c = self.pos
        block = self.index(1 - z, y, c)
        self.await_block(block)
        self.push(block, self.index(z, self.up, c))
        self.push(block, self.index(z, self.down, c))
        self.push(block, self.index(z, y, 1 - c))

    def ring(self, zz):
        s, z, y, c = self.pos
        block = self.index(zz, self.down, c)
        self.await_block(block)
        self.push(block, self.index(z, self.up, c))
        self.push(block, self.index(z, y, 1 - c))
        block = self.index(zz, self.up, c)
        self.await_block(block)
        self.push(block, self.index(z, y, 1 - c))

    def p2(self):
        self.ring(self.pos[1])

    def p3(self):
        self.ring(1 - self.pos[1])

    def p4(self):
        s, z, y, c = self.pos
        for zz in (z, 1 - z):
            block = self.index(zz, self.far, c)
            self.await_block(block)
            self.push(block, self.index(z, y, 1 - c))

    def p5(self):
        s, z, y, c = self.pos
        for zz in (z, 1 - z):
            for yy in (y, self.down, self.up, self.far):
                self.await_block(self.index(zz, yy, 1 - c))

    def finish(self):
        for copy in self.pending:
            copy.wait_send()


def kernel(
    tok, mod, wqkv1, wout1, wqkv2, wout2, wmi, wmo, out,
    tokr, tokf, g1, g2, g3, wo1, wo2, wc1, wc2,
    qb, kb, vb, o1b, o1f, qkvb, o2b, o2r, xb, acc,
    rs_send, rs_a, own_sum, rs_b, rs_c, rs_d, rs_e, mid_b, mid_c, mid_d, mid_e,
    res_s, res_r,
    tr_s, tr_r, tf_s, tf_r, o1_s, o1_r, o2_s, o2_r, re_s, re_r,
    g1_s, g1_r, g2_s, g2_r, g3_s, g3_r, w1_s, w1_r, w2_s, w2_r,
    ra_s, ra_r, rb_s, rb_r, rc_s, rc_r, rd_s, rd_r, re2_s, re2_r,
):
    s = lax.axis_index("seq")
    t = lax.axis_index("tp")
    z = lax.div(t, 8)
    y = lax.rem(lax.div(t, 2), 4)
    c = lax.rem(t, 2)
    pos = (s, z, y, c)
    diagonal = s == t

    def rows_of(i):
        return pl.ds(pl.multiple_of(i * BLK, BLK), BLK)

    barrier = pltpu.get_barrier_semaphore()

    def signal(dev):
        pl.semaphore_signal(barrier, inc=1, device_id=dev, device_id_type=pl.DeviceIdType.MESH)

    @pl.loop(1, N)
    def _(i):
        signal((s, lax.rem(t + i, N)))
        signal((lax.rem(s + i, N), s))
        signal((t, lax.rem(t + i, N)))

    @pl.when(jnp.logical_not(diagonal))
    def _():
        signal((s, s))
        signal((t, t))

    pl.semaphore_wait(barrier, 45 + jnp.where(diagonal, 0, 2))

    def tok_copy(i):
        peer = lax.rem(t + i, N)
        return remote(tok.at[rows_of(peer)], tokr.at[t], tr_s.at[i], tr_r.at[t], (s, peer))

    @pl.loop(1, N)
    def _(i):
        tok_copy(i).start()

    def far_copy(src, dst, ss, rs, i):
        r = lax.rem(s + i, N)
        return remote(src.at[rows_of(r)], dst.at[t], ss.at[i], rs.at[t], (r, s))

    def far_start(src, dst, ss, rs):
        @pl.when(jnp.logical_not(diagonal))
        def _():
            far_copy(src, dst, ss, rs, 0).start()

        @pl.when(diagonal)
        def _():
            dst[t] = src[rows_of(s), :]

        @pl.loop(1, N)
        def _(i):
            far_copy(src, dst, ss, rs, i).start()

    def far_wait_recv(src, dst, ss, rs):
        @pl.when(jnp.logical_not(diagonal))
        def _():
            remote(src.at[rows_of(0)], dst.at[t], ss.at[0], rs.at[t], (s, s)).wait_recv()

        @pl.loop(1, N)
        def _(i):
            k = lax.rem(t + i, N)
            remote(src.at[rows_of(0)], dst.at[k], ss.at[0], rs.at[k], (t, k)).wait_recv()

    def far_wait_send(src, dst, ss, rs):
        @pl.when(jnp.logical_not(diagonal))
        def _():
            far_copy(src, dst, ss, rs, 0).wait_send()

        @pl.loop(1, N)
        def _(i):
            far_copy(src, dst, ss, rs, i).wait_send()

    far_start(tok, tokf, tf_s, tf_r)
    tokr[t] = tok[rows_of(t), :]

    for j in range(3):
        wc1[:, j * HD:(j + 1) * HD] = wqkv1[j]
    for j in range(3):
        wc2[:, j * HD:(j + 1) * HD] = wqkv2[j]
    for w_in, w_all in ((wout1, wo1), (wout2, wo2)):
        w_all[t, 0:HD, :] = w_in[...]
        w_all[t, HD:PADW, :] = jnp.zeros((PADW - HD, D), BF)
    lanes = lax.broadcasted_iota(jnp.int32, (ROWS, 128), 1)
    vb[...] = jnp.where(lanes == HD, 1.0, 0.0).astype(BF)

    @pl.loop(1, N)
    def _(i):
        k = lax.rem(t + i, N)
        remote(tok.at[rows_of(0)], tokr.at[k], tr_s.at[0], tr_r.at[k], (s, k)).wait_recv()

    def side_by_side(blocks):
        for k in range(N):
            xb[:, k * HD:(k + 1) * HD] = blocks[k].astype(F32)

    side_by_side(tokr)

    def gather_of(buf, send, recv):
        return Gather(lambda i: buf.at[rows_of(i)], send, recv, pos)

    ga1 = gather_of(g1, g1_s, g1_r)
    g1[rows_of(t), :] = modulated(xb[...], mod[0:1, :], mod[1:2, :])
    ga1.p0()
    ga1.p1()
    ga1.p2()
    ga1.p3()
    ga1.p4()
    gw1 = Gather(lambda i: wo1.at[i], w1_s, w1_r, pos)
    gw1.p0()
    ga1.p5()

    @pl.loop(0, 3)
    def _(i):
        rows = pl.ds(pl.multiple_of(i * 256, 256), 256)
        r = jnp.dot(g1[rows, :], wc1[...], preferred_element_type=F32)
        qb[rows, :] = r[:, 0:HD].astype(BF)
        kb[rows, :] = r[:, HD:2 * HD].astype(BF)
        vb[rows, 0:HD] = r[:, 2 * HD:3 * HD].astype(BF)

    gw1.p1()
    gw1.p2()

    @pl.loop(0, 3)
    def _(i):
        rows = pl.ds(pl.multiple_of(i * 256, 256), 256)
        scores = lax.dot_general(
            qb[rows, :], kb[...], (((1,), (1,)), ((), ())), preferred_element_type=F32
        )
        top = jnp.max(scores, axis=1, keepdims=True)
        raised = jnp.exp((scores - top) * SCALE).astype(BF)
        mixed = jnp.dot(raised, vb[...], preferred_element_type=F32)
        o1b[rows, :] = (mixed[:, 0:HD] / mixed[:, HD:HD + 1]).astype(BF)

    far_start(o1b, o1f, o1_s, o1_r)
    gw1.p3()
    gw1.p4()
    far_wait_recv(tok, tokf, tf_s, tf_r)
    side_by_side(tokf)
    far_wait_recv(o1b, o1f, o1_s, o1_r)
    gw1.p5()

    def project(blocks, weights):
        acc[...] = jnp.zeros((BLK, D), F32)

        @pl.loop(0, N)
        def _(k):
            term = jnp.dot(blocks[k], weights[k, 0:HD, :], preferred_element_type=F32)
            acc[...] += term.astype(BF).astype(F32)

    project(o1f, wo1)
    x1 = (xb[...] + mod[2:3, :] * acc[...]).astype(BF).astype(F32)
    xb[...] = x1
    ga2 = gather_of(g2, g2_s, g2_r)
    g2[rows_of(t), :] = modulated(x1, mod[3:4, :], mod[4:5, :])
    ga2.p0()
    ga2.p1()
    ga2.p2()
    ga2.p3()
    ga2.p4()
    gw2 = Gather(lambda i: wo2.at[i], w2_s, w2_r, pos)
    gw2.p0()
    ga2.p5()

    @pl.loop(0, 3)
    def _(i):
        rows = pl.ds(pl.multiple_of(i * 256, 256), 256)
        r = jnp.dot(g2[rows, :], wc2[...], preferred_element_type=F32)
        qkvb[rows, :] = r.astype(BF)

    gw2.p1()
    gw2.p2()

    same = lax.rem(lax.broadcasted_iota(jnp.int32, (256, 256), 0), 16) == lax.rem(
        lax.broadcasted_iota(jnp.int32, (256, 256), 1), 16
    )
    for grp in range(3):
        part = jnp.concatenate(
            [qkvb[f * BLK + grp * 16:f * BLK + grp * 16 + 16, :] for f in range(N)], axis=0
        )
        q, k, v = part[:, 0:HD], part[:, HD:2 * HD], part[:, 2 * HD:3 * HD]
        scores = lax.dot_general(q, k, (((1,), (1,)), ((), ())), preferred_element_type=F32)
        scores = jnp.where(same, scores, -1e30)
        top = jnp.max(scores, axis=1, keepdims=True)
        raised = jnp.where(same, jnp.exp((scores - top) * SCALE), 0.0)
        weights = (raised / jnp.sum(raised, axis=1, keepdims=True)).astype(BF)
        mixed = jnp.dot(weights, v, preferred_element_type=F32).astype(BF)
        for f in range(N):
            o2b[f * BLK + grp * 16:f * BLK + grp * 16 + 16, :] = mixed[f * 16:f * 16 + 16, :]

    def o2_copy(i):
        peer = lax.rem(t + i, N)
        return remote(o2b.at[rows_of(peer)], o2r.at[t], o2_s.at[i], o2_r.at[t], (s, peer))

    @pl.loop(1, N)
    def _(i):
        o2_copy(i).start()

    o2r[t] = o2b[rows_of(t), :]
    gw2.p3()
    gw2.p4()

    @pl.loop(1, N)
    def _(i):
        k = lax.rem(t + i, N)
        remote(o2b.at[rows_of(0)], o2r.at[k], o2_s.at[0], o2_r.at[k], (s, k)).wait_recv()

    gw2.p5()
    project(o2r, wo2)
    x2 = (xb[...] + mod[5:6, :] * acc[...]).astype(BF).astype(F32)
    xb[...] = x2
    ga3 = gather_of(g3, g3_s, g3_r)
    g3[rows_of(t), :] = modulated(x2, mod[6:7, :], mod[7:8, :])
    ga3.p0()
    ga3.p1()
    ga3.p2()
    ga3.p3()
    ga3.p4()
    ga3.p5()

    def mlp(zz, cc):
        rows = jnp.concatenate([g3[rows_of(zz * 8 + yy * 2 + cc), :] for yy in range(4)], axis=0)
        hidden = jax.nn.gelu(
            jnp.dot(rows, wmi[...], preferred_element_type=F32), approximate=True
        ).astype(BF)
        return jnp.dot(hidden, wmo[...], preferred_element_type=F32)

    partner = (s, z * 8 + y * 2 + 1 - c)

    def ra_copy(j):
        return remote(rs_send.at[j], rs_a.at[j], ra_s.at[j], ra_r.at[j], partner)

    @pl.loop(0, 2)
    def _(zz):
        r = mlp(zz, 1 - c)
        for yy in range(4):
            rs_send[zz * 4 + yy] = r[yy * BLK:(yy + 1) * BLK, :].astype(BF)
            ra_copy(zz * 4 + yy).start()

    @pl.loop(0, 2)
    def _(zz):
        r = mlp(zz, c)
        for yy in range(4):
            own_sum[zz * 4 + yy] = r[yy * BLK:(yy + 1) * BLK, :]

    up = lax.rem(y + 1 + 2 * c, 4)
    down = lax.rem(y + 3 - 2 * c, 4)
    far = lax.rem(y + 2, 4)
    to_up = (s, z * 8 + up * 2 + c)
    to_down = (s, z * 8 + down * 2 + c)
    to_z = (s, (1 - z) * 8 + y * 2 + c)

    def chip_sum(zz, yy):
        ra_copy(zz * 4 + yy).wait_recv()
        return own_sum[zz * 4 + yy] + rs_a[zz * 4 + yy].astype(F32)

    def rb_copy(zz):
        return remote(mid_b.at[zz], rs_b.at[zz], rb_s.at[zz], rb_r.at[zz], to_up)

    def rc_copy(zz):
        return remote(mid_c.at[zz], rs_c.at[zz], rc_s.at[zz], rc_r.at[zz], to_down)

    def rd_copy(zz):
        return remote(mid_d.at[zz], rs_d.at[zz], rd_s.at[zz], rd_r.at[zz], to_up)

    for zz in range(2):
        mid_b[zz] = chip_sum(zz, far).astype(BF)
        rb_copy(zz).start()
    for zz in range(2):
        mid_c[zz] = chip_sum(zz, down).astype(BF)
        rc_copy(zz).start()
    for zz in range(2):
        r = chip_sum(zz, up)
        rb_copy(zz).wait_recv()
        mid_d[zz] = (r + rs_b[zz].astype(F32)).astype(BF)
        rd_copy(zz).start()
    for zz in range(2):
        own_sum[zz * 4 + y] = chip_sum(zz, y)
    for zz in range(2):
        rc_copy(zz).wait_recv()
        rd_copy(zz).wait_recv()
    mid_e[...] = (
        own_sum[(1 - z) * 4 + y] + rs_c[1 - z].astype(F32) + rs_d[1 - z].astype(F32)
    ).astype(BF)
    re_copy = remote(mid_e, rs_e, re2_s, re2_r, to_z)
    re_copy.start()
    mine = own_sum[z * 4 + y] + rs_c[z].astype(F32) + rs_d[z].astype(F32)
    re_copy.wait_recv()
    total = mine + rs_e[...].astype(F32)
    result = (xb[...] + mod[8:9, :] * total).astype(BF)
    for k in range(N):
        res_s[k] = result[:, k * HD:(k + 1) * HD]

    def res_copy(i):
        k = lax.rem(t + i, N)
        return remote(res_s.at[k], res_r.at[rows_of(s)], re_s.at[i], re_r.at[s], (t, k))

    @pl.when(jnp.logical_not(diagonal))
    def _():
        res_copy(0).start()

    @pl.when(diagonal)
    def _():
        res_r[rows_of(s), :] = res_s[t]

    @pl.loop(1, N)
    def _(i):
        res_copy(i).start()

    @pl.loop(1, N)
    def _(i):
        tok_copy(i).wait_send()
        o2_copy(i).wait_send()

    far_wait_send(tok, tokf, tf_s, tf_r)
    far_wait_send(o1b, o1f, o1_s, o1_r)
    for g in (ga1, ga2, ga3, gw1, gw2):
        g.finish()

    @pl.loop(0, 8)
    def _(j):
        ra_copy(j).wait_send()

    for zz in range(2):
        rb_copy(zz).wait_send()
        rc_copy(zz).wait_send()
        rd_copy(zz).wait_send()
    re_copy.wait_send()

    @pl.when(jnp.logical_not(diagonal))
    def _():
        res_copy(0).wait_send()
        remote(res_s.at[0], res_r.at[rows_of(s)], re_s.at[0], re_r.at[s], (s, s)).wait_recv()

    @pl.loop(1, N)
    def _(i):
        res_copy(i).wait_send()
        k = lax.rem(s + i, N)
        remote(res_s.at[0], res_r.at[rows_of(k)], re_s.at[0], re_r.at[k], (k, s)).wait_recv()

    out[...] = res_r[...]


def per_device(tokens, modulation, spatial_qkv, spatial_out, temporal_qkv, temporal_out, mlp_in, mlp_out):
    vm = pltpu.VMEM
    dma = pltpu.SemaphoreType.DMA
    scratch = [
        vm((N, BLK, HD), BF),
        vm((N, BLK, HD), BF),
        vm((ROWS, D), BF),
        vm((ROWS, D), BF),
        vm((ROWS, D), BF),
        vm((N, PADW, D), BF),
        vm((N, PADW, D), BF),
        vm((D, 3 * HD), BF),
        vm((D, 3 * HD), BF),
        vm((ROWS, HD), BF),
        vm((ROWS, HD), BF),
        vm((ROWS, 128), BF),
        vm((ROWS, HD), BF),
        vm((N, BLK, HD), BF),
        vm((ROWS, 3 * HD), BF),
        vm((ROWS, HD), BF),
        vm((N, BLK, HD), BF),
        vm((BLK, D), F32),
        vm((BLK, D), F32),
        vm((8, BLK, D), BF),
        vm((8, BLK, D), BF),
        vm((8, BLK, D), F32),
        vm((2, BLK, D), BF),
        vm((2, BLK, D), BF),
        vm((2, BLK, D), BF),
        vm((BLK, D), BF),
        vm((2, BLK, D), BF),
        vm((2, BLK, D), BF),
        vm((2, BLK, D), BF),
        vm((BLK, D), BF),
        vm((N, BLK, HD), BF),
        vm((ROWS, HD), BF),
    ]
    scratch += [dma((N,))] * 20
    scratch += [dma((8,)), dma((8,))] + [dma((2,))] * 6 + [dma, dma]
    return pl.pallas_call(
        kernel,
        out_shape=jax.ShapeDtypeStruct((ROWS, HD), BF),
        in_specs=[pl.BlockSpec(memory_space=pltpu.VMEM)] * 8,
        out_specs=pl.BlockSpec(memory_space=pltpu.VMEM),
        scratch_shapes=scratch,
        compiler_params=pltpu.CompilerParams(
            collective_id=0, has_side_effects=True, vmem_limit_bytes=50 * 1024 * 1024
        ),
        cost_estimate=pl.CostEstimate(
            flops=2_300_000_000, bytes_accessed=4_000_000, transcendentals=1_000_000
        ),
    )(tokens, modulation, spatial_qkv, spatial_out, temporal_qkv, temporal_out, mlp_in, mlp_out)


def solution(mesh):
    return jax.shard_map(
        per_device,
        mesh=mesh,
        in_specs=(
            P("seq", "tp"),
            P(),
            P(None, None, "tp"),
            P("tp", None),
            P(None, None, "tp"),
            P("tp", None),
            P(None, "tp"),
            P("tp", None),
        ),
        out_specs=P("seq", "tp"),
        check_vma=False,
    )
```

time: 391 us -> 138 us (0.35)
  waiting for transfers between devices: 299 us -> 0 us
  Pallas kernels: 3.48 us -> 131 us
  blocking collectives: 36.1 us -> 0 us
  matrix products: 15.8 us -> 0 us
  other arithmetic: 14.8 us -> 0 us
  between operations: 13.7 us -> 0.1 us
    reduce_scatter x3 -> x0, waiting for transfers between devices: 181 us -> none  [per_device(): lax.psum_scatter(partial_value.astype(jnp.bfloat16), 'tp', scatter_dimens...]
    pallas_call x0 -> x1, Pallas kernels: none -> 131 us  [per_device(): pl.pallas_call(kernel, out_shape=jax.ShapeDtypeStruct((ROWS, HD), BF), in...]
    all_gather x3 -> x0, waiting for transfers between devices: 117 us -> none  [the longest x1 41 us: per_device(): whole_rows = lax.all_gather(tokens, 'tp', axis=1, tiled=True)]
    all_to_all x2 -> x0, blocking collectives: 36.1 us -> none  [the longest x1 20 us: per_device(): lax.all_to_all(projected, 'seq', split_axis=2, concat_axis=1, tiled=True)]
    dot_general x11 -> x0, matrix products: 15.4 us -> none  [the longest x1 4.49 us: feed_forward(): return jnp.dot(hidden, mlp_out, preferred_element_type=jnp.float32)]
    reduce_sum x6 -> x0, other arithmetic: 7.32 us -> none  [the longest x3 5.76 us: modulated(): average = jnp.mean(as_float, axis=-1, keepdims=True)]
    convert_element_type x5 -> x0, other arithmetic: 6.26 us -> none  [the longest x3 4.93 us: residual_add(): return (base.astype(jnp.float32) + gate_row * update).astype(jnp.bfloat16)]
  transfers between devices with their start and end apart: 6 -> 0, of which waited for: 6 -> 0; matrix products, arithmetic and copies ran while one was open for 1% -> 0% of each run, Pallas kernels for 0% -> 0%
where the time goes in v1:
time: 138 us; the launch traced here: 137 us
  Pallas kernels  131 us (95%)
  local copies, waits for them, and re-layouts  6.43 us (5%)
    pallas_call x1, Pallas kernels, per_device(): pl.pallas_call(kernel, out_shape=jax.ShapeDtypeStruct((ROWS, HD), BF), in...  131 us
    unnamed x14, local copies, waits for them, and re-layouts  5.65 us

profile of v1, /device:TPU:1, one launch (start us, length us, event | category | flops | bytes accessed | tf_op | source)
XLA Modules:
  0.0 137.4 jit_solution(2729061454865220297)
XLA Ops:
  0.0 1.1 copy.9.tok
  1.1 0.0 copy-start.4
  1.1 1.5 %copy.10.wqkv1 = bf16[3,1152,72]{2,1,0:T(8,128)(2,1)S(1)} copy(bf16[3,1152,72]{1,2,0:T(8,128)(2,1)} %param.10) | data formatting | bytes 995328 | tf_op args[2]
  2.6 0.0 copy-done.4
  2.6 0.4 copy.11.wqkv2
  3.0 0.0 copy-start.1
  3.1 0.0 copy-start.2
  3.1 0.0 copy-start.3
  3.1 1.5 %copy.12.wmi = bf16[1152,288]{1,0:T(8,128)(2,1)S(1)} copy(bf16[1152,288]{0,1:T(8,128)(2,1)} %param.14) | data formatting | bytes 1327104 | tf_op args[6]
  4.6 0.0 copy-done.1
  4.6 0.0 copy-done.2
  4.6 0.0 copy-done.3
  4.7 0.0 copy-start
  4.7 1.1 copy-done
  5.7 130.9 %shard_map.82 = bf16[768,72]{1,0:T(8,128)(2,1)S(1)} custom-call(bf16[768,72]{1,0:T(8,128)(2,1)S(1)} %copy.9.tok, f32[9,1152]{1,0:T(8,128)S(1)} %copy-done.3, bf16[3,1152,72]{2,1,0:T(8,128)(2,1)S(1)} %copy.10.wqkv1, bf16[72,1152]{1,0:T(8,128)(2,1)S(1)} %copy-done.1, bf16[3,1152,72]{2,1,0:T(8,128)(2,1)S(1)} %copy.11.wqkv2, bf16[72,1152]{1,0:T(8,128)(2,1)S(1)} %copy-done.2, ...), custom_call_target="tpu_custom_call" | custom-call | flops 2300000000 | bytes 4000000 | tf_op jit(solution)/shard_map/pallas_call | solution.py:508
  136.6 0.8 copy.13
Async XLA Ops:
  1.1 1.5 %copy-start.4 = (bf16[3,1152,72]{1,2,0:T(8,128)(2,1)S(1)}, bf16[3,1152,72]{1,2,0:T(8,128)(2,1)}, u32[]{:S(2)}) copy-start(bf16[3,1152,72]{1,2,0:T(8,128)(2,1)} %param.12) | copy-start | bytes 1492996
  3.0 1.6 %copy-start.1 = (bf16[72,1152]{1,0:T(8,128)(2,1)S(1)}, bf16[72,1152]{1,0:T(8,128)(2,1)}, u32[]{:S(2)}) copy-start(bf16[72,1152]{1,0:T(8,128)(2,1)} %wout1.1) | copy-start | bytes 497668
  3.1 1.6 %copy-start.2 = (bf16[72,1152]{1,0:T(8,128)(2,1)S(1)}, bf16[72,1152]{1,0:T(8,128)(2,1)}, u32[]{:S(2)}) copy-start(bf16[72,1152]{1,0:T(8,128)(2,1)} %wout2.1) | copy-start | bytes 497668
  3.1 1.6 %copy-start.3 = (f32[9,1152]{1,0:T(8,128)S(1)}, f32[9,1152]{1,0:T(8,128)}, u32[]{:S(2)}) copy-start(f32[9,1152]{1,0:T(8,128)} %mod.1) | copy-start | bytes 124420
  4.7 1.1 copy-start

commit v2 on v0

v2 whole, which is shorter than its diff:
```python
import jax
import jax.numpy as jnp
from jax import lax
from jax.experimental import pallas as pl
from jax.experimental.pallas import tpu as pltpu
from jax.sharding import PartitionSpec as P

HD = 72
D = 1152
N = 16
ROWS = 768
BLK = 48
FFL = 288
PADW = 80
CUT = 48
SHARE = 80
EPS = 1e-06
SCALE = HD ** (-0.5)
BF = jnp.bfloat16
F32 = jnp.float32


def remote(src, dst, send_sem, recv_sem, device):
    return pltpu.make_async_remote_copy(
        src_ref=src,
        dst_ref=dst,
        send_sem=send_sem,
        recv_sem=recv_sem,
        device_id=device,
        device_id_type=pl.DeviceIdType.MESH,
    )


def dot_nt(a, b):
    return lax.dot_general(a, b, (((1,), (1,)), ((), ())), preferred_element_type=F32)


def modulated(rows, shift, scale):
    average = jnp.mean(rows, axis=-1, keepdims=True)
    centred = rows - average
    variance = jnp.mean(centred * centred, axis=-1, keepdims=True)
    return (centred * lax.rsqrt(variance + EPS) * (1.0 + scale) + shift).astype(BF)


class Copies:
    def __init__(self, send):
        self.send = send
        self.started = []

    def push(self, src, dst, recv, device):
        copy = remote(src, dst, self.send.at[len(self.started)], recv, device)
        copy.start()
        self.started.append(copy)

    def finish(self):
        for copy in self.started:
            copy.wait_send()


class Place:
    def __init__(self):
        self.s = lax.axis_index("seq")
        self.t = lax.axis_index("tp")
        self.z = lax.div(self.t, 8)
        self.y = lax.rem(lax.div(self.t, 2), 4)
        self.c = lax.rem(self.t, 2)
        self.zh = lax.div(self.s, 4)
        self.x = lax.rem(self.s, 4)
        self.up = lax.rem(self.y + 1, 4)
        self.down = lax.rem(self.y + 3, 4)
        self.far = lax.rem(self.y + 2, 4)

    def at(self, z, y, c):
        return z * 8 + y * 2 + c

    def dev(self, z, y, c):
        return (self.s, self.at(z, y, c))

    def partner(self):
        return self.dev(self.z, self.y, 1 - self.c)

    def z_inner(self):
        return self.dev(1 - self.z, self.y, self.c)

    def z_outer(self):
        zh = lax.rem(self.zh + jnp.where(self.z == 1, 1, 3), 4)
        return (zh * 4 + self.x, self.at(1 - self.z, self.y, self.c))


class Gather:
    def __init__(self, buf, send, recv, at, planes, chunks):
        self.buf, self.recv, self.p, self.planes, self.chunks = buf, recv, at, planes, chunks
        self.rows = BLK // chunks
        self.copies = Copies(send)

    def slot(self, o, k):
        if self.planes == 1:
            o = lax.rem(o, 8)
        return self.buf.at[pl.ds(pl.multiple_of(o * BLK + k * self.rows, self.rows), self.rows)]

    def sem(self, o, k):
        return self.recv.at[o, k]

    def push(self, o, k, device):
        ref = self.slot(o, k)
        self.copies.push(ref, ref, self.sem(o, k), device)

    def arrive(self, o, k):
        ref = self.slot(o, k)
        remote(ref, ref, self.copies.send.at[0], self.sem(o, k), self.p.partner()).wait_recv()

    def start(self):
        p = self.p
        for k in range(self.chunks):
            if self.planes == 2:
                self.push(p.t, k, p.z_inner())
            for yy in (p.up, p.down, p.far):
                self.push(p.t, k, p.dev(p.z, yy, p.c))
        for k in range(self.chunks):
            self.push(p.t, k, p.partner())

    def forward(self):
        p = self.p
        if self.planes == 1:
            return
        for k in range(self.chunks):
            o = p.at(1 - p.z, p.y, p.c)
            self.arrive(o, k)
            for yy in (p.up, p.down):
                self.push(o, k, p.dev(p.z, yy, p.c))
            self.push(o, k, p.partner())
        for k in range(self.chunks):
            o = p.at(p.z, p.far, p.c)
            self.arrive(o, k)
            self.push(o, k, p.z_inner())
            self.push(o, k, p.partner())

    def relay(self):
        p = self.p
        near = (p.up, p.down) if self.planes == 2 else (p.up, p.down, p.far)
        for k in range(self.chunks):
            for yy in near:
                o = p.at(p.z, yy, p.c)
                self.arrive(o, k)
                self.push(o, k, p.partner())
        if self.planes == 2:
            for k in range(self.chunks):
                for yy in (p.up, p.down, p.far):
                    o = p.at(1 - p.z, yy, p.c)
                    self.arrive(o, k)
                    self.push(o, k, p.partner())

    def complete(self):
        p = self.p
        for zz in (p.z, 1 - p.z)[: self.planes]:
            for yy in (p.y, p.up, p.down, p.far):
                for k in range(self.chunks):
                    self.arrive(p.at(zz, yy, 1 - p.c), k)


class WeightGather:
    def __init__(self, buf, send, recv, at):
        self.buf, self.recv, self.p = buf, recv, at
        self.copies = Copies(send)

    def part(self, o, h):
        return self.buf.at[o, pl.ds(0, CUT)] if h == 0 else self.buf.at[o, pl.ds(CUT, PADW - CUT)]

    def halves(self, o):
        p = self.p
        for h, device in ((0, p.z_inner()), (1, p.z_outer())):
            ref = self.part(o, h)
            self.copies.push(ref, ref, self.recv.at[o, h], device)

    def whole(self, o, device):
        ref = self.buf.at[o]
        self.copies.push(ref, ref, self.recv.at[o, 0], device)

    def arrive(self, o):
        ref = self.buf.at[o]
        remote(ref, ref, self.copies.send.at[0], self.recv.at[o, 0], self.p.partner()).wait_recv()

    def start_z(self):
        self.halves(self.p.t)

    def start_y(self):
        p = self.p
        for yy in (p.up, p.down, p.far):
            self.whole(p.t, p.dev(p.z, yy, p.c))
        self.whole(p.t, p.partner())

    def forward(self):
        p = self.p
        for yy in (p.up, p.down, p.far):
            o = p.at(p.z, yy, p.c)
            self.arrive(o)
            self.halves(o)
            self.whole(o, p.partner())

    def relay(self):
        p = self.p
        for yy in (p.y, p.up, p.down, p.far):
            o = p.at(1 - p.z, yy, p.c)
            for h in range(2):
                ref = self.part(o, h)
                remote(ref, ref, self.copies.send.at[0], self.recv.at[o, h], p.partner()).wait_recv()
            self.whole(o, p.partner())

    def complete(self):
        p = self.p
        for zz in (p.z, 1 - p.z):
            for yy in (p.y, p.up, p.down, p.far):
                self.arrive(p.at(zz, yy, 1 - p.c))


def kernel(
    tok_t, mod, wqkv1, wout1, wqkv2, wout2, wmi, wmo, out_t,
    tok, tokr, tokf, g1, g2, g3, wo1, wo2, wc1, wc2, wia, woa,
    qb, kb, vb, o1b, o1f, qkvb, o2b, o2r, xb, xp,
    rs_send, rs_a, own_sum, mid, rs_y, res_s, res_r,
    known_x, known_z,
    tr_s, tr_r, tf_s, tf_r, o1_s, o1_r, o2_s, o2_r, re_s, re_r,
    g1_s, g1_r, g2_s, g2_r, g3_s, g3_r, w1_s, w1_r, w2_s, w2_r, wm_s, wm_r, wl_s,
    ra_s, ra_r, ry_s, ry_r,
):
    p = Place()
    s, t = p.s, p.t
    frame = jnp.bitwise_xor(s, t)
    origin = t == 0

    def rows_of(i):
        return pl.ds(pl.multiple_of(i * BLK, BLK), BLK)

    def tell(sem, dev):
        pl.semaphore_signal(sem, inc=1, device_id=dev, device_id_type=pl.DeviceIdType.MESH)

    barrier = pltpu.get_barrier_semaphore()
    x_peers = [(p.zh * 4 + lax.rem(p.x + j, 4), t) for j in (1, 2, 3)]
    z_peers = [(lax.rem(p.zh + j, 4) * 4 + p.x, t) for j in (1, 2, 3)]

    for dev in x_peers + z_peers + [p.z_outer()]:
        tell(barrier, dev)

    @pl.loop(1, N)
    def _(i):
        tell(barrier, (s, lax.rem(t + i, N)))

    tok[...] = jnp.transpose(tok_t[...].astype(F32)).astype(BF)
    pl.semaphore_wait(barrier, 22)

    def tok_copy(i):
        peer = lax.rem(t + i, N)
        return remote(tok.at[rows_of(peer)], tokr.at[t], tr_s.at[i], tr_r.at[t], (s, peer))

    @pl.loop(1, N)
    def _(i):
        tok_copy(i).start()

    tokr[t] = tok[rows_of(t), :]
    for dev in x_peers:
        tell(known_x, dev)

    local = [
        pltpu.make_async_copy(wmi, wia.at[0], wl_s.at[0]),
        pltpu.make_async_copy(wmo, woa.at[0], wl_s.at[1]),
    ]
    for copy in local:
        copy.start()
    gw1 = WeightGather(wo1, w1_s, w1_r, p)
    gw2 = WeightGather(wo2, w2_s, w2_r, p)
    for w_in, w_all in ((wout1, wo1), (wout2, wo2)):
        w_all[t, 0:HD, :] = w_in[...]
        w_all[t, HD:PADW, :] = jnp.zeros((PADW - HD, D), BF)
    gw1.start_z()
    gw2.start_z()
    for w_in, w_all in ((wqkv1, wc1), (wqkv2, wc2)):
        w_all[...] = jnp.concatenate([w_in[j].astype(F32) for j in range(3)], axis=0).astype(BF)
    lanes = lax.broadcasted_iota(jnp.int32, (ROWS, 128), 1)
    vb[...] = jnp.where(lanes == HD, 1.0, 0.0).astype(BF)
    xp[...] = jnp.zeros((BLK, N * PADW), F32)

    @pl.loop(1, N)
    def _(i):
        k = lax.rem(t + i, N)
        remote(tok.at[rows_of(0)], tokr.at[k], tr_s.at[0], tr_r.at[k], (s, k)).wait_recv()

    def side_by_side(blocks):
        for k in range(N):
            xb[:, k * HD:(k + 1) * HD] = blocks[k].astype(F32)

    side_by_side(tokr)
    ga1 = Gather(g1, g1_s, g1_r, p, 2, 3)
    g1[rows_of(t), :] = modulated(xb[...], mod[0:1, :], mod[1:2, :])
    ga1.start()
    pl.semaphore_wait(known_x, 3)
    for dev in z_peers:
        tell(known_z, dev)
    ga1.forward()
    gw1.start_y()
    ga1.relay()
    pl.semaphore_wait(known_z, 3)

    def far_copy(src, dst, ss, rs, r):
        return remote(
            src.at[rows_of(r)], dst.at[t], ss.at[r], rs.at[t], (r, jnp.bitwise_xor(s, r))
        )

    def far_start(src, dst, ss, rs, r):
        own = jnp.logical_and(origin, r == s)

        @pl.when(jnp.logical_not(own))
        def _():
            far_copy(src, dst, ss, rs, r).start()

        @pl.when(own)
        def _():
            dst[t] = src[rows_of(s), :]

    def far_wait_recv(src, dst, ss, rs):
        @pl.loop(0, N)
        def _(i):
            k = lax.rem(t + i, N)

            @pl.when(jnp.logical_not(jnp.logical_and(origin, i == 0)))
            def _():
                remote(
                    src.at[rows_of(0)], dst.at[k], ss.at[0], rs.at[k], p.partner()
                ).wait_recv()

    def far_wait_send(src, dst, ss, rs):
        @pl.loop(0, N)
        def _(r):
            @pl.when(jnp.logical_not(jnp.logical_and(origin, r == s)))
            def _():
                far_copy(src, dst, ss, rs, r).wait_send()

    @pl.loop(0, N)
    def _(i):
        far_start(tok, tokf, tf_s, tf_r, lax.rem(s + i, N))

    ga1.complete()

    @pl.loop(0, 3)
    def _(i):
        rows = pl.ds(pl.multiple_of(i * 256, 256), 256)
        r = dot_nt(g1[rows, :], wc1[...])
        qb[rows, :] = r[:, 0:HD].astype(BF)
        kb[rows, :] = r[:, HD:2 * HD].astype(BF)
        vb[rows, 0:HD] = r[:, 2 * HD:3 * HD].astype(BF)

    @pl.loop(0, 4)
    def _(i):
        part = lax.rem(i + p.zh, 4)
        rows = pl.ds(pl.multiple_of(part * 192, 192), 192)
        scores = dot_nt(qb[rows, :], kb[...])
        top = jnp.max(scores, axis=1, keepdims=True)
        raised = jnp.exp((scores - top) * SCALE).astype(BF)
        mixed = jnp.dot(raised, vb[...], preferred_element_type=F32)
        o1b[rows, :] = (mixed[:, 0:HD] / mixed[:, HD:HD + 1]).astype(BF)
        for j in range(4):
            far_start(o1b, o1f, o1_s, o1_r, part * 4 + lax.rem(p.x + j, 4))

    gw2.start_y()
    gw1.forward()
    far_wait_recv(tok, tokf, tf_s, tf_r)
    side_by_side(tokf)
    gw1.relay()
    far_wait_recv(o1b, o1f, o1_s, o1_r)
    gw1.complete()

    def project(blocks, weights):
        for k in range(N):
            xp[:, k * PADW:k * PADW + HD] = blocks[k].astype(F32)
        return jnp.dot(
            xp[...].astype(BF), weights[...].reshape(N * PADW, D), preferred_element_type=F32
        )

    x1 = (xb[...] + mod[2:3, :] * project(o1f, wo1)).astype(BF).astype(F32)
    xb[...] = x1
    ga2 = Gather(g2, g2_s, g2_r, p, 2, 3)
    g2[rows_of(t), :] = modulated(x1, mod[3:4, :], mod[4:5, :])
    ga2.start()
    ga2.forward()
    gw2.forward()
    ga2.relay()

    mlp_copies = Copies(wm_s)
    for j, (w_in, w_all) in enumerate(((wmi, wia), (wmo, woa))):
        for h, (low, size, device) in enumerate(((0, SHARE, p.z_inner()), (SHARE, FFL - SHARE, p.z_outer()))):
            mlp_copies.push(
                w_in.at[pl.ds(low, size)], w_all.at[1, pl.ds(low, size)], wm_r.at[j, h], device
            )

    ga2.complete()

    @pl.loop(0, 3)
    def _(i):
        rows = pl.ds(pl.multiple_of(i * 256, 256), 256)
        qkvb[rows, :] = dot_nt(g2[rows, :], wc2[...]).astype(BF)

    same = lax.rem(lax.broadcasted_iota(jnp.int32, (256, 256), 0), 16) == lax.rem(
        lax.broadcasted_iota(jnp.int32, (256, 256), 1), 16
    )
    for grp in range(3):
        part = jnp.concatenate(
            [qkvb[f * BLK + grp * 16:f * BLK + grp * 16 + 16, :] for f in range(N)], axis=0
        )
        q, k, v = part[:, 0:HD], part[:, HD:2 * HD], part[:, 2 * HD:3 * HD]
        scores = jnp.where(same, dot_nt(q, k), -1e30)
        top = jnp.max(scores, axis=1, keepdims=True)
        raised = jnp.where(same, jnp.exp((scores - top) * SCALE), 0.0)
        weights = (raised / jnp.sum(raised, axis=1, keepdims=True)).astype(BF)
        mixed = jnp.dot(weights, v, preferred_element_type=F32).astype(BF)
        for f in range(N):
            o2b[f * BLK + grp * 16:f * BLK + grp * 16 + 16, :] = mixed[f * 16:f * 16 + 16, :]

    def o2_copy(i):
        peer = lax.rem(t + i, N)
        return remote(o2b.at[rows_of(peer)], o2r.at[t], o2_s.at[i], o2_r.at[t], (s, peer))

    @pl.loop(1, N)
    def _(i):
        o2_copy(i).start()

    o2r[t] = o2b[rows_of(t), :]
    gw2.relay()

    @pl.loop(1, N)
    def _(i):
        k = lax.rem(t + i, N)
        remote(o2b.at[rows_of(0)], o2r.at[k], o2_s.at[0], o2_r.at[k], (s, k)).wait_recv()

    gw2.complete()
    x2 = (xb[...] + mod[5:6, :] * project(o2r, wo2)).astype(BF).astype(F32)
    xb[...] = x2
    ga3 = Gather(g3, g3_s, g3_r, p, 1, 1)
    g3[rows_of(lax.rem(t, 8)), :] = modulated(x2, mod[6:7, :], mod[7:8, :])
    ga3.start()
    for copy in local:
        copy.wait()
    for j, w_all in enumerate((wia, woa)):
        for h, (low, size) in enumerate(((0, SHARE), (SHARE, FFL - SHARE))):
            ref = w_all.at[1, pl.ds(low, size)]
            remote(ref, ref, wm_s.at[0], wm_r.at[j, h], p.partner()).wait_recv()
    ga3.relay()
    ga3.complete()

    def mlp(cc):
        rows = jnp.concatenate([g3[rows_of(yy * 2 + cc), :] for yy in range(4)], axis=0)
        total = None
        for h in range(2):
            hidden = jax.nn.gelu(dot_nt(rows, wia[h]), approximate=True).astype(BF)
            term = jnp.dot(hidden, woa[h], preferred_element_type=F32)
            total = term if total is None else total + term
        return total

    def ra_copy(j):
        return remote(rs_send.at[j], rs_a.at[j], ra_s.at[j], ra_r.at[j], p.partner())

    r = mlp(1 - p.c)
    for yy in range(4):
        rs_send[yy] = r[yy * BLK:(yy + 1) * BLK, :].astype(BF)
        ra_copy(yy).start()
    r = mlp(p.c)
    for yy in range(4):
        own_sum[yy] = r[yy * BLK:(yy + 1) * BLK, :]

    def chip_sum(yy):
        ra_copy(yy).wait_recv()
        return own_sum[yy] + rs_a[yy].astype(F32)

    def ry_copy(j, yy):
        return remote(mid.at[j], rs_y.at[j], ry_s.at[j], ry_r.at[j], p.dev(p.z, yy, p.c))

    ring = (p.far, p.up, p.down)
    for j, yy in enumerate(ring):
        mid[j] = chip_sum(yy).astype(BF)
        ry_copy(j, yy).start()
    total = chip_sum(p.y)
    for j, yy in enumerate(ring):
        ry_copy(j, yy).wait_recv()
        total = total + rs_y[j].astype(F32)
    result = (xb[...] + mod[8:9, :] * total).astype(BF)
    for k in range(N):
        res_s[k] = result[:, k * HD:(k + 1) * HD]

    def res_copy(i):
        k = lax.rem(t + i, N)
        return remote(res_s.at[k], res_r.at[rows_of(s)], re_s.at[i], re_r.at[s], (frame, k))

    @pl.when(jnp.logical_not(origin))
    def _():
        res_copy(0).start()

    @pl.when(origin)
    def _():
        res_r[rows_of(s), :] = res_s[t]

    @pl.loop(1, N)
    def _(i):
        res_copy(i).start()

    @pl.loop(1, N)
    def _(i):
        tok_copy(i).wait_send()
        o2_copy(i).wait_send()

    far_wait_send(tok, tokf, tf_s, tf_r)
    far_wait_send(o1b, o1f, o1_s, o1_r)
    for g in (ga1, ga2, ga3, gw1, gw2):
        g.copies.finish()
    mlp_copies.finish()
    for yy in range(4):
        ra_copy(yy).wait_send()
    for j, yy in enumerate(ring):
        ry_copy(j, yy).wait_send()

    @pl.when(jnp.logical_not(origin))
    def _():
        res_copy(0).wait_send()
        remote(res_s.at[0], res_r.at[rows_of(s)], re_s.at[0], re_r.at[s], p.partner()).wait_recv()

    @pl.loop(1, N)
    def _(i):
        res_copy(i).wait_send()
        k = lax.rem(s + i, N)
        remote(res_s.at[0], res_r.at[rows_of(k)], re_s.at[0], re_r.at[k], p.partner()).wait_recv()

    out_t[...] = jnp.transpose(res_r[...].astype(F32)).astype(BF)


def per_device(tokens, modulation, spatial_qkv, spatial_out, temporal_qkv, temporal_out, mlp_in, mlp_out):
    vm = pltpu.VMEM
    dma = pltpu.SemaphoreType.DMA
    regular = pltpu.SemaphoreType.REGULAR
    scratch = [
        vm((ROWS, HD), BF),
        vm((N, BLK, HD), BF),
        vm((N, BLK, HD), BF),
        vm((ROWS, D), BF),
        vm((ROWS, D), BF),
        vm((ROWS // 2, D), BF),
        vm((N, PADW, D), BF),
        vm((N, PADW, D), BF),
        vm((3 * HD, D), BF),
        vm((3 * HD, D), BF),
        vm((2, FFL, D), BF),
        vm((2, FFL, D), BF),
        vm((ROWS, HD), BF),
        vm((ROWS, HD), BF),
        vm((ROWS, 128), BF),
        vm((ROWS, HD), BF),
        vm((N, BLK, HD), BF),
        vm((ROWS, 3 * HD), BF),
        vm((ROWS, HD), BF),
        vm((N, BLK, HD), BF),
        vm((BLK, D), F32),
        vm((BLK, N * PADW), F32),
        vm((4, BLK, D), BF),
        vm((4, BLK, D), BF),
        vm((4, BLK, D), F32),
        vm((3, BLK, D), BF),
        vm((3, BLK, D), BF),
        vm((N, BLK, HD), BF),
        vm((ROWS, HD), BF),
        regular,
        regular,
    ]
    scratch += [dma((N,))] * 10
    scratch += [dma((64,)), dma((N, 3))] * 3
    scratch += [dma((24,)), dma((N, 2))] * 2
    scratch += [dma((4,)), dma((2, 2)), dma((2,))]
    scratch += [dma((4,)), dma((4,)), dma((3,)), dma((3,))]
    return pl.pallas_call(
        kernel,
        out_shape=jax.ShapeDtypeStruct((HD, ROWS), BF),
        in_specs=[pl.BlockSpec(memory_space=pltpu.VMEM)] * 6
        + [pl.BlockSpec(memory_space=pl.ANY)] * 2,
        out_specs=pl.BlockSpec(memory_space=pltpu.VMEM),
        scratch_shapes=scratch,
        compiler_params=pltpu.CompilerParams(
            collective_id=0, has_side_effects=True, vmem_limit_bytes=50 * 1024 * 1024
        ),
        cost_estimate=pl.CostEstimate(
            flops=2_300_000_000, bytes_accessed=4_000_000, transcendentals=1_000_000
        ),
    )(
        tokens.T,
        modulation,
        jnp.swapaxes(spatial_qkv, 1, 2),
        spatial_out,
        jnp.swapaxes(temporal_qkv, 1, 2),
        temporal_out,
        mlp_in.T,
        mlp_out,
    ).T


def solution(mesh):
    return jax.shard_map(
        per_device,
        mesh=mesh,
        in_specs=(
            P("seq", "tp"),
            P(),
            P(None, None, "tp"),
            P("tp", None),
            P(None, None, "tp"),
            P("tp", None),
            P(None, "tp"),
            P("tp", None),
        ),
        out_specs=P("seq", "tp"),
        check_vma=False,
    )
```

time: 391 us -> 121 us (0.31)
  waiting for transfers between devices: 299 us -> 0 us
  Pallas kernels: 3.48 us -> 112 us
  blocking collectives: 36.1 us -> 0 us
  matrix products: 15.8 us -> 0 us
  other arithmetic: 14.8 us -> 0 us
  between operations: 13.7 us -> 0.02 us
    reduce_scatter x3 -> x0, waiting for transfers between devices: 181 us -> none  [per_device(): lax.psum_scatter(partial_value.astype(jnp.bfloat16), 'tp', scatter_dimens...]
    all_gather x3 -> x0, waiting for transfers between devices: 117 us -> none  [the longest x1 41 us: per_device(): whole_rows = lax.all_gather(tokens, 'tp', axis=1, tiled=True)]
    pallas_call x0 -> x1, Pallas kernels: none -> 112 us  [per_device(): pl.pallas_call(kernel, out_shape=jax.ShapeDtypeStruct((HD, ROWS), BF), in...]
    all_to_all x2 -> x0, blocking collectives: 36.1 us -> none  [the longest x1 20 us: per_device(): lax.all_to_all(projected, 'seq', split_axis=2, concat_axis=1, tiled=True)]
    dot_general x11 -> x0, matrix products: 15.4 us -> none  [the longest x1 4.49 us: feed_forward(): return jnp.dot(hidden, mlp_out, preferred_element_type=jnp.float32)]
    reduce_sum x6 -> x0, other arithmetic: 7.32 us -> none  [the longest x3 5.76 us: modulated(): average = jnp.mean(as_float, axis=-1, keepdims=True)]
    convert_element_type x5 -> x0, other arithmetic: 6.26 us -> none  [the longest x3 4.93 us: residual_add(): return (base.astype(jnp.float32) + gate_row * update).astype(jnp.bfloat16)]
    unnamed x27 -> x17, local copies, waits for them, and re-layouts: 2.75 us -> 8.5 us
  transfers between devices with their start and end apart: 6 -> 0, of which waited for: 6 -> 0; matrix products, arithmetic and copies ran while one was open for 1% -> 0% of each run, Pallas kernels for 0% -> 0%
where the time goes in v2:
time: 121 us
  Pallas kernels  112 us (93%)
  local copies, waits for them, and re-layouts  8.5 us (7%)
    pallas_call x1, Pallas kernels, per_device(): pl.pallas_call(kernel, out_shape=jax.ShapeDtypeStruct((HD, ROWS), BF), in...  112 us
    unnamed x17, local copies, waits for them, and re-layouts  8.5 us

profile of v2, /device:TPU:1, one launch (start us, length us, event | category | flops | bytes accessed | tf_op | source)
XLA Modules:
  0.0 120.7 jit_solution(4719082591763304505)
XLA Ops:
  0.0 0.0 copy-start
  0.0 1.1 copy-done
  1.1 0.0 copy-start.1
  1.1 1.1 copy-done.1
  2.2 0.0 copy-start.2
  2.2 1.0 copy-done.2
  3.2 0.0 copy-start.3
  3.2 1.0 copy-done.3
  4.2 0.0 copy-start.4
  4.2 0.9 copy-done.4
  5.2 0.0 copy-start.5
  5.2 0.9 copy-done.5
  6.1 0.0 copy-start.6
  6.1 0.9 copy-done.6
  7.0 0.0 copy-start.7
  7.0 0.9 copy-done.7
  7.9 112.1 %shard_map.82 = bf16[72,768]{1,0:T(8,128)(2,1)S(1)} custom-call(bf16[72,768]{1,0:T(8,128)(2,1)S(1)} %bitcast.9, f32[9,1152]{1,0:T(8,128)S(1)} %copy-done.7, bf16[3,72,1152]{2,1,0:T(8,128)(2,1)S(1)} %bitcast.7, bf16[72,1152]{1,0:T(8,128)(2,1)S(1)} %copy-done.4, bf16[3,72,1152]{2,1,0:T(8,128)(2,1)S(1)} %bitcast.8, bf16[72,1152]{1,0:T(8,128)(2,1)S(1)} %copy-done.5, ...), custom_call_target="tpu_custom_call" | custom-call | flops 2300000000 | bytes 4000000 | tf_op jit(solution)/shard_map/pallas_call | solution.py:574
  120.0 0.6 copy.10
Async XLA Ops:
  0.0 1.1 copy-start
  1.1 1.1 copy-start.1
  2.2 1.0 copy-start.2
  3.2 1.0 copy-start.3
  4.2 0.9 copy-start.4
  5.2 0.9 copy-start.5
  6.1 0.9 copy-start.6
  7.0 0.9 copy-start.7

commit v3 on v2

--- a/solution.py
+++ b/solution.py
@@ -10,10 +10,11 @@
 N = 16
 ROWS = 768
 BLK = 48
+PK = 32
 FFL = 288
 PADW = 80
 CUT = 48
-SHARE = 80
+SHARE = 144
 EPS = 1e-06
 SCALE = HD ** (-0.5)
 BF = jnp.bfloat16
@@ -40,6 +41,19 @@
     centred = rows - average
     variance = jnp.mean(centred * centred, axis=-1, keepdims=True)
     return (centred * lax.rsqrt(variance + EPS) * (1.0 + scale) + shift).astype(BF)
+
+
+def pack(dst, i, block):
+    dst[i, :, 0:HD] = block[0:PK, :]
+    dst[i, 0:16, HD:128] = block[PK:BLK, 0:128 - HD]
+    dst[i, 16:PK, HD:2 * HD - 56] = block[PK:BLK, 56:HD]
+
+
+def unpack(dst, row, low, src, i):
+    block = src[i].astype(F32)
+    dst[row:row + PK, low:low + HD] = block[:, 0:HD]
+    dst[row + PK:row + BLK, low:low + 56] = block[0:16, HD:128]
+    dst[row + PK:row + BLK, low + 56:low + HD] = block[16:PK, HD:2 * HD - 56]
 
 
 class Copies:
@@ -180,20 +194,29 @@
         ref = self.buf.at[o]
         remote(ref, ref, self.copies.send.at[0], self.recv.at[o, 0], self.p.partner()).wait_recv()
 
+    def arrive_parts(self, o):
+        for h in range(2):
+            ref = self.part(o, h)
+            remote(
+                ref, ref, self.copies.send.at[0], self.recv.at[o, h], self.p.partner()
+            ).wait_recv()
+
     def start_z(self):
         self.halves(self.p.t)
 
-    def start_y(self):
-        p = self.p
-        for yy in (p.up, p.down, p.far):
-            self.whole(p.t, p.dev(p.z, yy, p.c))
-        self.whole(p.t, p.partner())
+    def start_y(self, h):
+        p = self.p
+        ref = self.part(p.t, h)
+        for yy in (p.far, p.up, p.down):
+            self.copies.push(ref, ref, self.recv.at[p.t, h], p.dev(p.z, yy, p.c))
+        if h == 0:
+            self.whole(p.t, p.partner())
 
     def forward(self):
         p = self.p
         for yy in (p.up, p.down, p.far):
             o = p.at(p.z, yy, p.c)
-            self.arrive(o)
+            self.arrive_parts(o)
             self.halves(o)
             self.whole(o, p.partner())
 
@@ -201,9 +224,7 @@
         p = self.p
         for yy in (p.y, p.up, p.down, p.far):
             o = p.at(1 - p.z, yy, p.c)
-            for h in range(2):
-                ref = self.part(o, h)
-                remote(ref, ref, self.copies.send.at[0], self.recv.at[o, h], p.partner()).wait_recv()
+            self.arrive_parts(o)
             self.whole(o, p.partner())
 
     def complete(self):
@@ -214,9 +235,9 @@
 
 
 def kernel(
-    tok_t, mod, wqkv1, wout1, wqkv2, wout2, wmi, wmo, out_t,
-    tok, tokr, tokf, g1, g2, g3, wo1, wo2, wc1, wc2, wia, woa,
-    qb, kb, vb, o1b, o1f, qkvb, o2b, o2r, xb, xp,
+    tok_h, mod_h, wqkv1_h, wout1_h, wqkv2_h, wout2_h, wmi_h, wmo_h, out_t,
+    tok_t, mod, wqkv1, wout1, wqkv2, wout2, tok, tokr, x0b, x0f, g1, g2, g3, wo1, wo2, wc1, wc2, wia, woa,
+    qb, kb, vb, o1b, o1f, qkvb, o2b, o2p, o2r, xb, xp, rows_f,
     rs_send, rs_a, own_sum, mid, rs_y, res_s, res_r,
     known_x, known_z,
     tr_s, tr_r, tf_s, tf_r, o1_s, o1_r, o2_s, o2_r, re_s, re_r,
@@ -234,6 +255,24 @@
     def tell(sem, dev):
         pl.semaphore_signal(sem, inc=1, device_id=dev, device_id_type=pl.DeviceIdType.MESH)
 
+    inward = [
+        pltpu.make_async_copy(src, dst, wl_s.at[j])
+        for j, (src, dst) in enumerate(
+            (
+                (tok_h, tok_t),
+                (mod_h, mod),
+                (wout1_h, wout1),
+                (wout2_h, wout2),
+                (wqkv1_h, wqkv1),
+                (wqkv2_h, wqkv2),
+                (wmi_h, wia.at[0]),
+                (wmo_h, woa.at[0]),
+            )
+        )
+    ]
+    for copy in inward:
+        copy.start()
+
     barrier = pltpu.get_barrier_semaphore()
     x_peers = [(p.zh * 4 + lax.rem(p.x + j, 4), t) for j in (1, 2, 3)]
     z_peers = [(lax.rem(p.zh + j, 4) * 4 + p.x, t) for j in (1, 2, 3)]
@@ -245,33 +284,33 @@
     def _(i):
         tell(barrier, (s, lax.rem(t + i, N)))
 
-    tok[...] = jnp.transpose(tok_t[...].astype(F32)).astype(BF)
+    inward[0].wait()
+    rows = jnp.transpose(tok_t[...].astype(F32)).astype(BF)
+    for k in range(N):
+        pack(tok, k, rows[k * BLK:(k + 1) * BLK, :])
     pl.semaphore_wait(barrier, 22)
 
     def tok_copy(i):
         peer = lax.rem(t + i, N)
-        return remote(tok.at[rows_of(peer)], tokr.at[t], tr_s.at[i], tr_r.at[t], (s, peer))
+        return remote(tok.at[peer], tokr.at[t], tr_s.at[i], tr_r.at[t], (s, peer))
 
     @pl.loop(1, N)
     def _(i):
         tok_copy(i).start()
 
-    tokr[t] = tok[rows_of(t), :]
+    tokr[t] = tok[t]
     for dev in x_peers:
         tell(known_x, dev)
 
-    local = [
-        pltpu.make_async_copy(wmi, wia.at[0], wl_s.at[0]),
-        pltpu.make_async_copy(wmo, woa.at[0], wl_s.at[1]),
-    ]
-    for copy in local:
-        copy.start()
+    for copy in inward[1:6]:
+        copy.wait()
     gw1 = WeightGather(wo1, w1_s, w1_r, p)
     gw2 = WeightGather(wo2, w2_s, w2_r, p)
     for w_in, w_all in ((wout1, wo1), (wout2, wo2)):
         w_all[t, 0:HD, :] = w_in[...]
         w_all[t, HD:PADW, :] = jnp.zeros((PADW - HD, D), BF)
     gw1.start_z()
+    gw1.start_y(1)
     gw2.start_z()
     for w_in, w_all in ((wqkv1, wc1), (wqkv2, wc2)):
         w_all[...] = jnp.concatenate([w_in[j].astype(F32) for j in range(3)], axis=0).astype(BF)
@@ -282,13 +321,14 @@
     @pl.loop(1, N)
     def _(i):
         k = lax.rem(t + i, N)
-        remote(tok.at[rows_of(0)], tokr.at[k], tr_s.at[0], tr_r.at[k], (s, k)).wait_recv()
+        remote(tok.at[0], tokr.at[k], tr_s.at[0], tr_r.at[k], (s, k)).wait_recv()
 
     def side_by_side(blocks):
         for k in range(N):
-            xb[:, k * HD:(k + 1) * HD] = blocks[k].astype(F32)
+            unpack(xb, 0, k * HD, blocks, k)
 
     side_by_side(tokr)
+    x0b[...] = xb[...].astype(BF)
     ga1 = Gather(g1, g1_s, g1_r, p, 2, 3)
     g1[rows_of(t), :] = modulated(xb[...], mod[0:1, :], mod[1:2, :])
     ga1.start()
@@ -296,13 +336,13 @@
     for dev in z_peers:
         tell(known_z, dev)
     ga1.forward()
-    gw1.start_y()
+    gw1.start_y(0)
     ga1.relay()
     pl.semaphore_wait(known_z, 3)
 
     def far_copy(src, dst, ss, rs, r):
         return remote(
-            src.at[rows_of(r)], dst.at[t], ss.at[r], rs.at[t], (r, jnp.bitwise_xor(s, r))
+            src.at[r], dst.at[t], ss.at[r], rs.at[t], (r, jnp.bitwise_xor(s, r))
         )
 
     def far_start(src, dst, ss, rs, r):
@@ -314,7 +354,7 @@
 
         @pl.when(own)
         def _():
-            dst[t] = src[rows_of(s), :]
+            dst[t] = src[s]
 
     def far_wait_recv(src, dst, ss, rs):
         @pl.loop(0, N)
@@ -324,7 +364,7 @@
             @pl.when(jnp.logical_not(jnp.logical_and(origin, i == 0)))
             def _():
                 remote(
-                    src.at[rows_of(0)], dst.at[k], ss.at[0], rs.at[k], p.partner()
+                    src.at[0], dst.at[k], ss.at[0], rs.at[k], p.partner()
                 ).wait_recv()
 
     def far_wait_send(src, dst, ss, rs):
@@ -334,9 +374,16 @@
             def _():
                 far_copy(src, dst, ss, rs, r).wait_send()
 
-    @pl.loop(0, N)
-    def _(i):
-        far_start(tok, tokf, tf_s, tf_r, lax.rem(s + i, N))
+    corner = jnp.logical_and(s == 0, t == 0)
+    row_copy = remote(x0b, x0f, tf_s, tf_r, (t, frame))
+
+    @pl.when(jnp.logical_not(corner))
+    def _():
+        row_copy.start()
+
+    @pl.when(corner)
+    def _():
+        x0f[...] = x0b[...]
 
     ga1.complete()
 
@@ -356,26 +403,31 @@
         top = jnp.max(scores, axis=1, keepdims=True)
         raised = jnp.exp((scores - top) * SCALE).astype(BF)
         mixed = jnp.dot(raised, vb[...], preferred_element_type=F32)
-        o1b[rows, :] = (mixed[:, 0:HD] / mixed[:, HD:HD + 1]).astype(BF)
+        mixed = (mixed[:, 0:HD] / mixed[:, HD:HD + 1]).astype(BF)
+        for j in range(4):
+            pack(o1b, part * 4 + j, mixed[j * BLK:(j + 1) * BLK, :])
         for j in range(4):
             far_start(o1b, o1f, o1_s, o1_r, part * 4 + lax.rem(p.x + j, 4))
 
-    gw2.start_y()
+    gw2.start_y(1)
+    gw2.start_y(0)
     gw1.forward()
-    far_wait_recv(tok, tokf, tf_s, tf_r)
-    side_by_side(tokf)
+    @pl.when(jnp.logical_not(corner))
+    def _():
+        row_copy.wait_recv()
+
     gw1.relay()
     far_wait_recv(o1b, o1f, o1_s, o1_r)
     gw1.complete()
 
     def project(blocks, weights):
         for k in range(N):
-            xp[:, k * PADW:k * PADW + HD] = blocks[k].astype(F32)
+            unpack(xp, 0, k * PADW, blocks, k)
         return jnp.dot(
             xp[...].astype(BF), weights[...].reshape(N * PADW, D), preferred_element_type=F32
         )
 
-    x1 = (xb[...] + mod[2:3, :] * project(o1f, wo1)).astype(BF).astype(F32)
+    x1 = (x0f[...].astype(F32) + mod[2:3, :] * project(o1f, wo1)).astype(BF).astype(F32)
     xb[...] = x1
     ga2 = Gather(g2, g2_s, g2_r, p, 2, 3)
     g2[rows_of(t), :] = modulated(x1, mod[3:4, :], mod[4:5, :])
@@ -383,13 +435,6 @@
     ga2.forward()
     gw2.forward()
     ga2.relay()
-
-    mlp_copies = Copies(wm_s)
-    for j, (w_in, w_all) in enumerate(((wmi, wia), (wmo, woa))):
-        for h, (low, size, device) in enumerate(((0, SHARE, p.z_inner()), (SHARE, FFL - SHARE, p.z_outer()))):
-            mlp_copies.push(
-                w_in.at[pl.ds(low, size)], w_all.at[1, pl.ds(low, size)], wm_r.at[j, h], device
-            )
 
     ga2.complete()
 
@@ -414,21 +459,33 @@
         for f in range(N):
             o2b[f * BLK + grp * 16:f * BLK + grp * 16 + 16, :] = mixed[f * 16:f * 16 + 16, :]
 
+    for f in range(N):
+        pack(o2p, f, o2b[f * BLK:(f + 1) * BLK, :])
+
     def o2_copy(i):
         peer = lax.rem(t + i, N)
-        return remote(o2b.at[rows_of(peer)], o2r.at[t], o2_s.at[i], o2_r.at[t], (s, peer))
+        return remote(o2p.at[peer], o2r.at[t], o2_s.at[i], o2_r.at[t], (s, peer))
 
     @pl.loop(1, N)
     def _(i):
         o2_copy(i).start()
 
-    o2r[t] = o2b[rows_of(t), :]
+    o2r[t] = o2p[t]
+    for copy in inward[6:]:
+        copy.wait()
+    mlp_copies = Copies(wm_s)
+    for j, w_all in enumerate((wia, woa)):
+        for h, (low, size, device) in enumerate(((0, SHARE, p.z_inner()), (SHARE, FFL - SHARE, p.z_outer()))):
+            mlp_copies.push(
+                w_all.at[0, pl.ds(low, size)], w_all.at[1, pl.ds(low, size)], wm_r.at[j, h], device
+            )
+
     gw2.relay()
 
     @pl.loop(1, N)
     def _(i):
         k = lax.rem(t + i, N)
-        remote(o2b.at[rows_of(0)], o2r.at[k], o2_s.at[0], o2_r.at[k], (s, k)).wait_recv()
+        remote(o2p.at[0], o2r.at[k], o2_s.at[0], o2_r.at[k], (s, k)).wait_recv()
 
     gw2.complete()
     x2 = (xb[...] + mod[5:6, :] * project(o2r, wo2)).astype(BF).astype(F32)
@@ -436,8 +493,6 @@
     ga3 = Gather(g3, g3_s, g3_r, p, 1, 1)
     g3[rows_of(lax.rem(t, 8)), :] = modulated(x2, mod[6:7, :], mod[7:8, :])
     ga3.start()
-    for copy in local:
-        copy.wait()
     for j, w_all in enumerate((wia, woa)):
         for h, (low, size) in enumerate(((0, SHARE), (SHARE, FFL - SHARE))):
             ref = w_all.at[1, pl.ds(low, size)]
@@ -482,11 +537,11 @@
         total = total + rs_y[j].astype(F32)
     result = (xb[...] + mod[8:9, :] * total).astype(BF)
     for k in range(N):
-        res_s[k] = result[:, k * HD:(k + 1) * HD]
+        pack(res_s, k, result[:, k * HD:(k + 1) * HD])
 
     def res_copy(i):
         k = lax.rem(t + i, N)
-        return remote(res_s.at[k], res_r.at[rows_of(s)], re_s.at[i], re_r.at[s], (frame, k))
+        return remote(res_s.at[k], res_r.at[s], re_s.at[i], re_r.at[s], (frame, k))
 
     @pl.when(jnp.logical_not(origin))
     def _():
@@ -494,7 +549,7 @@
 
     @pl.when(origin)
     def _():
-        res_r[rows_of(s), :] = res_s[t]
+        res_r[s] = res_s[t]
 
     @pl.loop(1, N)
     def _(i):
@@ -505,7 +560,10 @@
         tok_copy(i).wait_send()
         o2_copy(i).wait_send()
 
-    far_wait_send(tok, tokf, tf_s, tf_r)
+    @pl.when(jnp.logical_not(corner))
+    def _():
+        row_copy.wait_send()
+
     far_wait_send(o1b, o1f, o1_s, o1_r)
     for g in (ga1, ga2, ga3, gw1, gw2):
         g.copies.finish()
@@ -518,15 +576,17 @@
     @pl.when(jnp.logical_not(origin))
     def _():
         res_copy(0).wait_send()
-        remote(res_s.at[0], res_r.at[rows_of(s)], re_s.at[0], re_r.at[s], p.partner()).wait_recv()
+        remote(res_s.at[0], res_r.at[s], re_s.at[0], re_r.at[s], p.partner()).wait_recv()
 
     @pl.loop(1, N)
     def _(i):
         res_copy(i).wait_send()
         k = lax.rem(s + i, N)
-        remote(res_s.at[0], res_r.at[rows_of(k)], re_s.at[0], re_r.at[k], p.partner()).wait_recv()
-
-    out_t[...] = jnp.transpose(res_r[...].astype(F32)).astype(BF)
+        remote(res_s.at[0], res_r.at[k], re_s.at[0], re_r.at[k], p.partner()).wait_recv()
+
+    for k in range(N):
+        unpack(rows_f, k * BLK, 0, res_r, k)
+    out_t[...] = jnp.transpose(rows_f[...]).astype(BF)
 
 
 def per_device(tokens, modulation, spatial_qkv, spatial_out, temporal_qkv, temporal_out, mlp_in, mlp_out):
@@ -534,9 +594,16 @@
     dma = pltpu.SemaphoreType.DMA
     regular = pltpu.SemaphoreType.REGULAR
     scratch = [
-        vm((ROWS, HD), BF),
-        vm((N, BLK, HD), BF),
-        vm((N, BLK, HD), BF),
+        vm((HD, ROWS), BF),
+        vm((9, D), F32),
+        vm((3, HD, D), BF),
+        vm((HD, D), BF),
+        vm((3, HD, D), BF),
+        vm((HD, D), BF),
+        vm((N, PK, 128), BF),
+        vm((N, PK, 128), BF),
+        vm((BLK, D), BF),
+        vm((BLK, D), BF),
         vm((ROWS, D), BF),
         vm((ROWS, D), BF),
         vm((ROWS // 2, D), BF),
@@ -549,37 +616,38 @@
         vm((ROWS, HD), BF),
         vm((ROWS, HD), BF),
         vm((ROWS, 128), BF),
-        vm((ROWS, HD), BF),
-        vm((N, BLK, HD), BF),
+        vm((N, PK, 128), BF),
+        vm((N, PK, 128), BF),
         vm((ROWS, 3 * HD), BF),
         vm((ROWS, HD), BF),
-        vm((N, BLK, HD), BF),
+        vm((N, PK, 128), BF),
+        vm((N, PK, 128), BF),
         vm((BLK, D), F32),
         vm((BLK, N * PADW), F32),
+        vm((ROWS, HD), F32),
         vm((4, BLK, D), BF),
         vm((4, BLK, D), BF),
         vm((4, BLK, D), F32),
         vm((3, BLK, D), BF),
         vm((3, BLK, D), BF),
-        vm((N, BLK, HD), BF),
-        vm((ROWS, HD), BF),
+        vm((N, PK, 128), BF),
+        vm((N, PK, 128), BF),
         regular,
         regular,
     ]
-    scratch += [dma((N,))] * 10
+    scratch += [dma((N,))] * 2 + [dma, dma] + [dma((N,))] * 6
     scratch += [dma((64,)), dma((N, 3))] * 3
     scratch += [dma((24,)), dma((N, 2))] * 2
-    scratch += [dma((4,)), dma((2, 2)), dma((2,))]
+    scratch += [dma((4,)), dma((2, 2)), dma((8,))]
     scratch += [dma((4,)), dma((4,)), dma((3,)), dma((3,))]
     return pl.pallas_call(
         kernel,
         out_shape=jax.ShapeDtypeStruct((HD, ROWS), BF),
-        in_specs=[pl.BlockSpec(memory_space=pltpu.VMEM)] * 6
-        + [pl.BlockSpec(memory_space=pl.ANY)] * 2,
+        in_specs=[pl.BlockSpec(memory_space=pltpu.HBM)] * 8,
         out_specs=pl.BlockSpec(memory_space=pltpu.VMEM),
         scratch_shapes=scratch,
         compiler_params=pltpu.CompilerParams(
-            collective_id=0, has_side_effects=True, vmem_limit_bytes=50 * 1024 * 1024
+            collective_id=0, has_side_effects=True, vmem_limit_bytes=60 * 1024 * 1024
         ),
         cost_estimate=pl.CostEstimate(
             flops=2_300_000_000, bytes_accessed=4_000_000, transcendentals=1_000_000

time: 121 us -> 105 us (0.87)
  Pallas kernels: 112 us -> 103 us
  local copies, waits for them, and re-layouts: 8.5 us -> 1.55 us
    pallas_call x1, Pallas kernels: 112 us -> 103 us  [per_device(): pl.pallas_call(kernel, out_shape=jax.ShapeDtypeStruct((HD, ROWS), BF), in...]
    unnamed x17 -> x1, local copies, waits for them, and re-layouts: 8.5 us -> 1.55 us
where the time goes in v3:
time: 105 us
  Pallas kernels  103 us (98%)
  local copies, waits for them, and re-layouts  1.55 us (1%)
    pallas_call x1, Pallas kernels, per_device(): pl.pallas_call(kernel, out_shape=jax.ShapeDtypeStruct((HD, ROWS), BF), in...  103 us

profile of v3, /device:TPU:1, one launch (start us, length us, event | category | flops | bytes accessed | tf_op | source)
XLA Modules:
  0.0 105.0 jit_solution(17392721638428326774)
XLA Ops:
  0.0 103.4 %shard_map.82 = bf16[72,768]{1,0:T(8,128)(2,1)} custom-call(bf16[72,768]{1,0:T(8,128)(2,1)} %bitcast.9, f32[9,1152]{1,0:T(8,128)} %mod_h.1, bf16[3,72,1152]{2,1,0:T(8,128)(2,1)} %bitcast.7, bf16[72,1152]{1,0:T(8,128)(2,1)} %wout1_h.1, bf16[3,72,1152]{2,1,0:T(8,128)(2,1)} %bitcast.8, bf16[72,1152]{1,0:T(8,128)(2,1)} %wout2_h.1, bf16[288,1152]{1,0:T(8,128)(2,1)} %bitcast.6, ...), custom_call_target="tpu_custom_call" | custom-call | flops 2300000000 | bytes 4000000 | tf_op jit(solution)/shard_map/pallas_call | solution.py:643
  103.4 1.5 %copy.10 = bf16[768,72]{0,1:T(8,128)(2,1)} copy(bf16[768,72]{0,1:T(8,128)(2,1)} %bitcast.5) | data formatting | bytes 221184

commit v4 on v3

--- a/solution.py
+++ b/solution.py
@@ -14,7 +14,7 @@
 FFL = 288
 PADW = 80
 CUT = 48
-SHARE = 144
+MLP_PARTS = ((0, 144, True), (144, 64, True), (208, 80, False))
 EPS = 1e-06
 SCALE = HD ** (-0.5)
 BF = jnp.bfloat16
@@ -309,6 +309,22 @@
     for w_in, w_all in ((wout1, wo1), (wout2, wo2)):
         w_all[t, 0:HD, :] = w_in[...]
         w_all[t, HD:PADW, :] = jnp.zeros((PADW - HD, D), BF)
+    for copy in inward[6:]:
+        copy.wait()
+    mlp_copies = Copies(wm_s)
+
+    def mlp_parts(parts):
+        for low, size, outer in parts:
+            for j, w_all in enumerate((wia, woa)):
+                rows = pl.ds(low, size)
+                sem = wm_r.at[j, low // 48]
+                yield w_all.at[0, rows], w_all.at[1, rows], sem, p.z_outer() if outer else p.z_inner()
+
+    def mlp_send(parts):
+        for copy in mlp_parts(parts):
+            mlp_copies.push(*copy)
+
+    mlp_send(MLP_PARTS[:1])
     gw1.start_z()
     gw1.start_y(1)
     gw2.start_z()
@@ -471,15 +487,7 @@
         o2_copy(i).start()
 
     o2r[t] = o2p[t]
-    for copy in inward[6:]:
-        copy.wait()
-    mlp_copies = Copies(wm_s)
-    for j, w_all in enumerate((wia, woa)):
-        for h, (low, size, device) in enumerate(((0, SHARE, p.z_inner()), (SHARE, FFL - SHARE, p.z_outer()))):
-            mlp_copies.push(
-                w_all.at[0, pl.ds(low, size)], w_all.at[1, pl.ds(low, size)], wm_r.at[j, h], device
-            )
-
+    mlp_send(MLP_PARTS[1:])
     gw2.relay()
 
     @pl.loop(1, N)
@@ -493,10 +501,8 @@
     ga3 = Gather(g3, g3_s, g3_r, p, 1, 1)
     g3[rows_of(lax.rem(t, 8)), :] = modulated(x2, mod[6:7, :], mod[7:8, :])
     ga3.start()
-    for j, w_all in enumerate((wia, woa)):
-        for h, (low, size) in enumerate(((0, SHARE), (SHARE, FFL - SHARE))):
-            ref = w_all.at[1, pl.ds(low, size)]
-            remote(ref, ref, wm_s.at[0], wm_r.at[j, h], p.partner()).wait_recv()
+    for src, dst, sem, _ in mlp_parts(MLP_PARTS):
+        remote(src, dst, wm_s.at[0], sem, p.partner()).wait_recv()
     ga3.relay()
     ga3.complete()
 
@@ -638,7 +644,7 @@
     scratch += [dma((N,))] * 2 + [dma, dma] + [dma((N,))] * 6
     scratch += [dma((64,)), dma((N, 3))] * 3
     scratch += [dma((24,)), dma((N, 2))] * 2
-    scratch += [dma((4,)), dma((2, 2)), dma((8,))]
+    scratch += [dma((6,)), dma((2, 6)), dma((8,))]
     scratch += [dma((4,)), dma((4,)), dma((3,)), dma((3,))]
     return pl.pallas_call(
         kernel,

time: 105 us -> 102 us (0.971)
  Pallas kernels: 103 us -> 100 us
    pallas_call x1, Pallas kernels: 103 us -> 100 us  [per_device(): pl.pallas_call(kernel, out_shape=jax.ShapeDtypeStruct((HD, ROWS), BF), in...]
where the time goes in v4:
time: 102 us
  Pallas kernels  100 us (98%)
  local copies, waits for them, and re-layouts  1.55 us (2%)
    pallas_call x1, Pallas kernels, per_device(): pl.pallas_call(kernel, out_shape=jax.ShapeDtypeStruct((HD, ROWS), BF), in...  100 us

profile of v4, /device:TPU:1, one launch (start us, length us, event | category | flops | bytes accessed | tf_op | source)
XLA Modules:
  0.0 101.9 jit_solution(16468629911284947509)
XLA Ops:
  0.0 100.3 %shard_map.82 = bf16[72,768]{1,0:T(8,128)(2,1)} custom-call(bf16[72,768]{1,0:T(8,128)(2,1)} %bitcast.9, f32[9,1152]{1,0:T(8,128)} %mod_h.1, bf16[3,72,1152]{2,1,0:T(8,128)(2,1)} %bitcast.7, bf16[72,1152]{1,0:T(8,128)(2,1)} %wout1_h.1, bf16[3,72,1152]{2,1,0:T(8,128)(2,1)} %bitcast.8, bf16[72,1152]{1,0:T(8,128)(2,1)} %wout2_h.1, bf16[288,1152]{1,0:T(8,128)(2,1)} %bitcast.6, ...), custom_call_target="tpu_custom_call" | custom-call | flops 2300000000 | bytes 4000000 | tf_op jit(solution)/shard_map/pallas_call | solution.py:649
  100.4 1.5 %copy.10 = bf16[768,72]{0,1:T(8,128)(2,1)} copy(bf16[768,72]{0,1:T(8,128)(2,1)} %bitcast.5) | data formatting | bytes 221184

commit v5 on v4

--- a/solution.py
+++ b/solution.py
@@ -324,10 +324,10 @@
         for copy in mlp_parts(parts):
             mlp_copies.push(*copy)
 
-    mlp_send(MLP_PARTS[:1])
     gw1.start_z()
     gw1.start_y(1)
     gw2.start_z()
+    mlp_send(MLP_PARTS[:1])
     for w_in, w_all in ((wqkv1, wc1), (wqkv2, wc2)):
         w_all[...] = jnp.concatenate([w_in[j].astype(F32) for j in range(3)], axis=0).astype(BF)
     lanes = lax.broadcasted_iota(jnp.int32, (ROWS, 128), 1)
@@ -498,7 +498,7 @@
     gw2.complete()
     x2 = (xb[...] + mod[5:6, :] * project(o2r, wo2)).astype(BF).astype(F32)
     xb[...] = x2
-    ga3 = Gather(g3, g3_s, g3_r, p, 1, 1)
+    ga3 = Gather(g3, g3_s, g3_r, p, 1, 3)
     g3[rows_of(lax.rem(t, 8)), :] = modulated(x2, mod[6:7, :], mod[7:8, :])
     ga3.start()
     for src, dst, sem, _ in mlp_parts(MLP_PARTS):

time: 102 us -> 101 us (level)
    pallas_call x1, Pallas kernels: 100 us -> 99.3 us  [per_device(): pl.pallas_call(kernel, out_shape=jax.ShapeDtypeStruct((HD, ROWS), BF), in...]
where the time goes in v5:
time: 101 us
  Pallas kernels  99.3 us (98%)
  local copies, waits for them, and re-layouts  1.55 us (2%)
    pallas_call x1, Pallas kernels, per_device(): pl.pallas_call(kernel, out_shape=jax.ShapeDtypeStruct((HD, ROWS), BF), in...  99.3 us

profile of v5, /device:TPU:1, one launch (start us, length us, event | category | flops | bytes accessed | tf_op | source)
XLA Modules:
  0.0 100.9 jit_solution(5099888741286892396)
XLA Ops:
  0.0 99.3 %shard_map.82 = bf16[72,768]{1,0:T(8,128)(2,1)} custom-call(bf16[72,768]{1,0:T(8,128)(2,1)} %bitcast.9, f32[9,1152]{1,0:T(8,128)} %mod_h.1, bf16[3,72,1152]{2,1,0:T(8,128)(2,1)} %bitcast.7, bf16[72,1152]{1,0:T(8,128)(2,1)} %wout1_h.1, bf16[3,72,1152]{2,1,0:T(8,128)(2,1)} %bitcast.8, bf16[72,1152]{1,0:T(8,128)(2,1)} %wout2_h.1, bf16[288,1152]{1,0:T(8,128)(2,1)} %bitcast.6, ...), custom_call_target="tpu_custom_call" | custom-call | flops 2300000000 | bytes 4000000 | tf_op jit(solution)/shard_map/pallas_call | solution.py:649
  99.3 1.5 %copy.10 = bf16[768,72]{0,1:T(8,128)(2,1)} copy(bf16[768,72]{0,1:T(8,128)(2,1)} %bitcast.5) | data formatting | bytes 221184

commit v6 on v5

--- a/solution.py
+++ b/solution.py
@@ -328,11 +328,6 @@
     gw1.start_y(1)
     gw2.start_z()
     mlp_send(MLP_PARTS[:1])
-    for w_in, w_all in ((wqkv1, wc1), (wqkv2, wc2)):
-        w_all[...] = jnp.concatenate([w_in[j].astype(F32) for j in range(3)], axis=0).astype(BF)
-    lanes = lax.broadcasted_iota(jnp.int32, (ROWS, 128), 1)
-    vb[...] = jnp.where(lanes == HD, 1.0, 0.0).astype(BF)
-    xp[...] = jnp.zeros((BLK, N * PADW), F32)
 
     @pl.loop(1, N)
     def _(i):
@@ -348,6 +343,9 @@
     ga1 = Gather(g1, g1_s, g1_r, p, 2, 3)
     g1[rows_of(t), :] = modulated(xb[...], mod[0:1, :], mod[1:2, :])
     ga1.start()
+    wc1[...] = jnp.concatenate([wqkv1[j].astype(F32) for j in range(3)], axis=0).astype(BF)
+    lanes = lax.broadcasted_iota(jnp.int32, (ROWS, 128), 1)
+    vb[...] = jnp.where(lanes == HD, 1.0, 0.0).astype(BF)
     pl.semaphore_wait(known_x, 3)
     for dev in z_peers:
         tell(known_z, dev)
@@ -413,7 +411,8 @@
 
     @pl.loop(0, 4)
     def _(i):
-        part = lax.rem(i + p.zh, 4)
+        ahead = jnp.where(i == 0, 2, jnp.where(i == 1, 1, jnp.where(i == 2, 3, 0)))
+        part = lax.rem(p.zh + ahead, 4)
         rows = pl.ds(pl.multiple_of(part * 192, 192), 192)
         scores = dot_nt(qb[rows, :], kb[...])
         top = jnp.max(scores, axis=1, keepdims=True)
@@ -422,12 +421,14 @@
         mixed = (mixed[:, 0:HD] / mixed[:, HD:HD + 1]).astype(BF)
         for j in range(4):
             pack(o1b, part * 4 + j, mixed[j * BLK:(j + 1) * BLK, :])
-        for j in range(4):
+        for j in (2, 1, 3, 0):
             far_start(o1b, o1f, o1_s, o1_r, part * 4 + lax.rem(p.x + j, 4))
 
     gw2.start_y(1)
     gw2.start_y(0)
     gw1.forward()
+    wc2[...] = jnp.concatenate([wqkv2[j].astype(F32) for j in range(3)], axis=0).astype(BF)
+    xp[...] = jnp.zeros((BLK, N * PADW), F32)
     @pl.when(jnp.logical_not(corner))
     def _():
         row_copy.wait_recv()

time: 101 us -> 102 us (level)
  no operation moved by 1% of the time
where the time goes in v6:
time: 102 us; the launch traced here: 101 us
  Pallas kernels  99.9 us (98%)
  local copies, waits for them, and re-layouts  1.55 us (2%)
    pallas_call x1, Pallas kernels, per_device(): pl.pallas_call(kernel, out_shape=jax.ShapeDtypeStruct((HD, ROWS), BF), in...  99.9 us

profile of v6, /device:TPU:1, one launch (start us, length us, event | category | flops | bytes accessed | tf_op | source)
XLA Modules:
  0.0 101.4 jit_solution(9061868119911381614)
XLA Ops:
  0.0 99.9 %shard_map.82 = bf16[72,768]{1,0:T(8,128)(2,1)} custom-call(bf16[72,768]{1,0:T(8,128)(2,1)} %bitcast.9, f32[9,1152]{1,0:T(8,128)} %mod_h.1, bf16[3,72,1152]{2,1,0:T(8,128)(2,1)} %bitcast.7, bf16[72,1152]{1,0:T(8,128)(2,1)} %wout1_h.1, bf16[3,72,1152]{2,1,0:T(8,128)(2,1)} %bitcast.8, bf16[72,1152]{1,0:T(8,128)(2,1)} %wout2_h.1, bf16[288,1152]{1,0:T(8,128)(2,1)} %bitcast.6, ...), custom_call_target="tpu_custom_call" | custom-call | flops 2300000000 | bytes 4000000 | tf_op jit(solution)/shard_map/pallas_call | solution.py:650
  99.9 1.5 %copy.10 = bf16[768,72]{0,1:T(8,128)(2,1)} copy(bf16[768,72]{0,1:T(8,128)(2,1)} %bitcast.5) | data formatting | bytes 221184
